TPU v7x, 32 devices: a whole 2x2x4 slice. The times are simulated.
32 devices in a mesh: dp: 8 (over y, x, core), tensor: 4 (over z).
Axes of the slice: x: 2, y: 2, z: 4, core: 2. Of those that a mesh axis runs over, the one named last changes fastest.
Arguments:
- tokens: bfloat16 [4096, 768], P(('dp', 'tensor')), may hold values from -6 to 6
- cotangent: bfloat16 [4096, 768], P(('dp', 'tensor')), may hold values from -6 to 6
- routes: int32 [4096, 1], P('dp'), may hold values from 0 to 3; in each aligned block of 512 rows (0 to 511, 512 to 1023, ...) at most 144 rows name the same one
- buckets: int32 [1023], replicated, may hold values from 0 to 31
- attn_gain: bfloat16 [768], P('dp'), may hold values from 0.099609375 to 1.8984375
- ffn_gain: bfloat16 [768], P('dp'), may hold values from 0.099609375 to 1.8984375
- w_query: bfloat16 [768, 768], P('dp', 'tensor'), may hold values from -0.078125 to 0.078125
- w_key: bfloat16 [768, 768], P('dp', 'tensor'), may hold values from -0.078125 to 0.078125
- w_value: bfloat16 [768, 768], P('dp', 'tensor'), may hold values from -0.21875 to 0.21875
- w_output: bfloat16 [768, 768], P('dp', 'tensor'), may hold values from -1.75 to 1.75
- rel_table: bfloat16 [12, 32], P('tensor'), may hold values from -4 to 4
- w_router: bfloat16 [768, 4], P('dp'), may hold values from -0.15625 to 0.15625
- expert_up: bfloat16 [4, 768, 3072], P(None, 'dp', 'tensor'), may hold values from -0.21875 to 0.21875
- expert_down: bfloat16 [4, 768, 3072], P(None, 'dp', 'tensor'), may hold values from -0.625 to 0.625
Outputs:
- layer_out: bfloat16 [4096, 768], P(('dp', 'tensor'))
- grad_tokens: float32 [4096, 768], P(('dp', 'tensor'))
- grad_attn_gain: float32 [768], P('dp')
- grad_ffn_gain: float32 [768], P('dp')
- grad_query: float32 [768, 768], P('dp', 'tensor')
- grad_key: float32 [768, 768], P('dp', 'tensor')
- grad_value: float32 [768, 768], P('dp', 'tensor')
- grad_output: float32 [768, 768], P('dp', 'tensor')
- grad_table: float32 [12, 32], P('tensor')
- grad_router: float32 [768, 4], P('dp')
- grad_up: float32 [4, 768, 3072], P(None, 'dp', 'tensor')
- grad_down: float32 [4, 768, 3072], P(None, 'dp', 'tensor')
Inputs may be any that keep to these rules, and one draw needn't show every extreme that they name: `routes`: in each sequence (512 aligned rows, the rows of one index of dp) no expert is named by more than 144 tokens, a bound that some block reaches.
All inputs are finite; a program needn't handle non-finite values.
Results may differ from a plain program's by a relative error of at most 0.015.
Values may be sent and summed in bfloat16 or wider, within the bound.
A program may use at most 128 MiB of HBM per device.

v0:
```python
import jax
import jax.numpy as jnp
from jax import lax
from jax.sharding import PartitionSpec as P

HEADS = 12
CAP = 144


epsilon = 1e-06
highest = lax.Precision.HIGHEST


def rms_norm(tok_rows, scale_vec):
    return (
        tok_rows
        * lax.rsqrt(jnp.mean(tok_rows * tok_rows, axis=-1, keepdims=True) + epsilon)
        * scale_vec
    )


def slot_targets(route_ids, experts, capacity):
    one_hot = (route_ids[:, None] == jnp.arange(experts, dtype=jnp.int32)[None, :]).astype(
        jnp.int32
    )
    before = jnp.cumsum(one_hot, axis=0) - one_hot
    slot_index = jnp.sum(before * one_hot, axis=1)
    return route_ids * capacity + slot_index


def ffn_front(hidden, scale_vec, router_mat, chosen):
    normed = rms_norm(hidden, scale_vec)
    logits = jnp.dot(normed, router_mat, precision=highest)
    gating = jnp.sum(jax.nn.softmax(logits, axis=-1) * chosen, axis=-1)
    return (normed, gating)


def gelu_tanh(pre_act):
    return jax.nn.gelu(pre_act, approximate=True)


def block_bias(rel_bias, block_rows, length):
    heads_here = rel_bias.shape[0]
    width = length + block_rows
    segment = rel_bias
    segment = jnp.pad(segment, ((0, 0), (0, 1)))
    tiled = jnp.broadcast_to(segment[:, None, :], (heads_here, block_rows, width)).reshape(
        heads_here, block_rows * width
    )
    skewed = tiled[:, block_rows - 1 : block_rows - 1 + block_rows * (width - 1)].reshape(
        heads_here, block_rows, width - 1
    )
    return skewed[:, :, :length]


def block_scores(queries, key_rows, rel_bias, length):
    block_rows = queries.shape[0]
    scores = jnp.einsum("ihd,jhd->hij", queries, key_rows, preferred_element_type=jnp.float32)
    return scores + block_bias(rel_bias, block_rows, length)


def diagonal_sums(score_block, length):
    heads_here = score_block.shape[0]
    block_rows = score_block.shape[1]
    padded = jnp.pad(score_block, ((0, 0), (0, 0), (block_rows, 0)))
    flattened = padded.reshape(heads_here, block_rows * (length + block_rows))
    flattened = jnp.pad(flattened, ((0, 0), (0, block_rows)))
    skewed = flattened.reshape(heads_here, block_rows, length + block_rows + 1)
    totals = jnp.sum(skewed, axis=1)[:, 1 : length + block_rows]
    return totals


def per_device(
    tokens,
    cotangent,
    routes,
    buckets,
    attn_gain,
    ffn_gain,
    w_query,
    w_key,
    w_value,
    w_output,
    rel_table,
    w_router,
    expert_up,
    expert_down,
):
    local_rows = tokens.shape[0]
    length = local_rows * lax.axis_size("tensor")
    heads_here = rel_table.shape[0]
    head_width = w_query.shape[1]
    head_size = head_width // heads_here
    experts = expert_up.shape[0]
    block_rows = min(512, length)
    gain_one, gain_two, router_full, query_full, key_full, value_full, output_full = (
        lax.all_gather(attn_gain, "dp", axis=0, tiled=True),
        lax.all_gather(ffn_gain, "dp", axis=0, tiled=True),
        lax.all_gather(w_router, "dp", axis=0, tiled=True),
        lax.all_gather(w_query, "dp", axis=0, tiled=True),
        lax.all_gather(w_key, "dp", axis=0, tiled=True),
        lax.all_gather(w_value, "dp", axis=0, tiled=True),
        lax.all_gather(w_output, "dp", axis=0, tiled=True),
    )
    proj_weights = jnp.concatenate([query_full, key_full, value_full], axis=1)
    router_mat = router_full.astype(jnp.float32)
    token_rows = tokens.astype(jnp.float32)
    normed_one, norm_back = jax.vjp(rms_norm, token_rows, gain_one.astype(jnp.float32))
    rows_all = lax.all_gather(normed_one.astype(jnp.bfloat16), "tensor", axis=0, tiled=True)
    projected = jnp.dot(rows_all, proj_weights, preferred_element_type=jnp.float32).astype(
        jnp.bfloat16
    )
    queries = projected[:, :head_width].reshape(length, heads_here, head_size)
    key_rows = projected[:, head_width : 2 * head_width].reshape(length, heads_here, head_size)
    value_rows = projected[:, 2 * head_width :].reshape(length, heads_here, head_size)
    table_vals = rel_table.astype(jnp.float32)
    bucket_hot = (
        buckets[:, None] == jnp.arange(table_vals.shape[1], dtype=jnp.int32)[None, :]
    ).astype(jnp.float32)
    rel_bias = jnp.dot(table_vals, bucket_hot.T, precision=highest)
    scores = block_scores(queries, key_rows, rel_bias, length)
    row_peak = jnp.max(scores, axis=-1, keepdims=True)
    log_total = row_peak + jnp.log(jnp.sum(jnp.exp(scores - row_peak), axis=-1, keepdims=True))
    weights_low = jnp.exp(scores - log_total).astype(jnp.bfloat16)
    ctx_block = jnp.einsum(
        "hij,jhd->ihd", weights_low, value_rows, preferred_element_type=jnp.float32
    )
    ctx_list = ctx_block.astype(jnp.bfloat16).reshape(block_rows, head_width)
    lse_list = [log_total]
    selected = ctx_list
    attended = lax.psum_scatter(
        lax.dot_general(
            selected, output_full, (((1,), (1,)), ((), ())), preferred_element_type=jnp.float32
        ),
        "tensor",
        scatter_dimension=0,
        tiled=True,
    )
    hidden = token_rows + attended
    route_all = routes[:, 0]
    route_mine = lax.dynamic_slice_in_dim(
        route_all, lax.axis_index("tensor") * local_rows, local_rows
    )
    chosen = (route_mine[:, None] == jnp.arange(experts, dtype=jnp.int32)[None, :]).astype(
        jnp.float32
    )
    (normed_two, gating), front_back = jax.vjp(
        lambda hidden_in, scale_in, router_in: ffn_front(hidden_in, scale_in, router_in, chosen),
        hidden,
        gain_two.astype(jnp.float32),
        router_mat,
    )
    ffn_all = lax.all_gather(normed_two.astype(jnp.bfloat16), "tensor", axis=0, tiled=True)
    targets = slot_targets(route_all, experts, CAP)
    model_dim = ffn_all.shape[1]
    dispatched = (
        jnp.zeros((experts * CAP, model_dim), jnp.bfloat16)
        .at[targets]
        .set(ffn_all)
        .reshape(experts, CAP, model_dim)
    )
    up_full, down_full = (
        lax.all_gather(expert_up, "dp", axis=1, tiled=True),
        lax.all_gather(expert_down, "dp", axis=1, tiled=True),
    )
    pre_act = jnp.einsum("ecd,edf->ecf", dispatched, up_full, preferred_element_type=jnp.float32)
    activated = gelu_tanh(pre_act).astype(jnp.bfloat16)
    expert_rows = jnp.einsum(
        "ecf,edf->ecd", activated, down_full, preferred_element_type=jnp.float32
    ).reshape(experts * CAP, model_dim)
    returned = lax.psum_scatter(expert_rows[targets], "tensor", scatter_dimension=0, tiled=True)
    layer_out = (hidden + gating[:, None] * returned).astype(jnp.bfloat16)
    grad_out = cotangent.astype(jnp.float32)
    grad_returned = (gating[:, None] * grad_out).astype(jnp.bfloat16)
    grad_gating = jnp.sum(grad_out * returned, axis=-1)
    grad_all = lax.all_gather(grad_returned, "tensor", axis=0, tiled=True)
    up_back, down_back = (up_full, down_full)
    grad_slots = (
        jnp.zeros((experts * CAP, model_dim), jnp.bfloat16)
        .at[targets]
        .set(grad_all)
        .reshape(experts, CAP, model_dim)
    )
    grad_act = jnp.einsum("ecd,edf->ecf", grad_slots, down_back, preferred_element_type=jnp.float32)
    grad_down = jnp.einsum(
        "ecd,ecf->edf", grad_slots, activated, preferred_element_type=jnp.float32
    )
    gelu_back = jax.vjp(gelu_tanh, pre_act)[1]
    grad_pre = gelu_back(grad_act)[0].astype(jnp.bfloat16)
    grad_up = jnp.einsum("ecd,ecf->edf", dispatched, grad_pre, preferred_element_type=jnp.float32)
    grad_disp = jnp.einsum(
        "ecf,edf->ecd", grad_pre, up_back, preferred_element_type=jnp.float32
    ).reshape(experts * CAP, model_dim)
    grad_normed_two = lax.psum_scatter(
        grad_disp[targets], "tensor", scatter_dimension=0, tiled=True
    )
    grad_hidden, grad_gain_two, grad_router = front_back((grad_normed_two, grad_gating))
    grad_hidden = grad_hidden + grad_out
    grad_att_all = lax.all_gather(grad_hidden.astype(jnp.bfloat16), "tensor", axis=0, tiled=True)
    grad_context = jnp.dot(grad_att_all, output_full, preferred_element_type=jnp.float32).astype(
        jnp.bfloat16
    )
    grad_output = lax.dot_general(
        grad_att_all, ctx_list, (((0,), (0,)), ((), ())), preferred_element_type=jnp.float32
    )
    grad_keys = jnp.zeros((length, heads_here, head_size), jnp.float32)
    grad_values = jnp.zeros((length, heads_here, head_size), jnp.float32)
    grad_rel = jnp.zeros((heads_here, 2 * length - 1), jnp.float32)
    query_grads = []
    for block_index, first_row in enumerate(range(0, length, block_rows)):
        scores = block_scores(queries, key_rows, rel_bias, length)
        weights_full = jnp.exp(scores - lse_list[block_index])
        weights_low = weights_full.astype(jnp.bfloat16)
        ctx_grad = grad_context.reshape(block_rows, heads_here, head_size)
        grad_weights = jnp.einsum(
            "ihd,jhd->hij", ctx_grad, value_rows, preferred_element_type=jnp.float32
        )
        inner_sum = jnp.sum(weights_full * grad_weights, axis=-1, keepdims=True)
        grad_scores = (weights_full * (grad_weights - inner_sum)).astype(jnp.bfloat16)
        query_grad = jnp.einsum(
            "hij,jhd->ihd", grad_scores, key_rows, preferred_element_type=jnp.float32
        )
        query_grads.append(query_grad.astype(jnp.bfloat16).reshape(block_rows, head_width))
        grad_keys = jnp.einsum(
            "hij,ihd->jhd", grad_scores, queries, preferred_element_type=jnp.float32
        )
        grad_values = jnp.einsum(
            "hij,ihd->jhd", weights_low, ctx_grad, preferred_element_type=jnp.float32
        )
        grad_rel = diagonal_sums(grad_scores.astype(jnp.float32), length)
    grad_proj = jnp.concatenate(
        [
            query_grads[0],
            grad_keys.astype(jnp.bfloat16).reshape(length, head_width),
            grad_values.astype(jnp.bfloat16).reshape(length, head_width),
        ],
        axis=1,
    )
    grad_table_here = jnp.dot(grad_rel, bucket_hot, precision=highest)
    grad_proj_w = lax.dot_general(
        rows_all, grad_proj, (((0,), (0,)), ((), ())), preferred_element_type=jnp.float32
    )
    selected = grad_proj
    grad_normed_one = lax.psum_scatter(
        lax.dot_general(
            selected, proj_weights, (((1,), (1,)), ((), ())), preferred_element_type=jnp.float32
        ).astype(jnp.bfloat16),
        "tensor",
        scatter_dimension=0,
        tiled=True,
    ).astype(jnp.float32)
    grad_rows_in, grad_gain_one = norm_back(grad_normed_one)
    grad_tokens = grad_hidden + grad_rows_in
    sum_query, sum_key, sum_value, sum_output = (
        lax.psum_scatter(grad_proj_w[:, :head_width], "dp", scatter_dimension=0, tiled=True),
        lax.psum_scatter(
            grad_proj_w[:, head_width : 2 * head_width], "dp", scatter_dimension=0, tiled=True
        ),
        lax.psum_scatter(grad_proj_w[:, 2 * head_width :], "dp", scatter_dimension=0, tiled=True),
        lax.psum_scatter(grad_output, "dp", scatter_dimension=0, tiled=True),
    )
    owners = lax.axis_size("dp")
    shard_model = model_dim // owners
    hidden_here = grad_up.shape[2]
    traded_up, traded_down = (
        lax.all_to_all(
            grad_up.astype(jnp.bfloat16), "dp", split_axis=1, concat_axis=0, tiled=True
        ).astype(grad_up.dtype),
        lax.all_to_all(
            grad_down.astype(jnp.bfloat16), "dp", split_axis=1, concat_axis=0, tiled=True
        ).astype(grad_down.dtype),
    )
    sum_up = jnp.sum(traded_up.reshape(owners, experts, shard_model, hidden_here), axis=0)
    sum_down = jnp.sum(traded_down.reshape(owners, experts, shard_model, hidden_here), axis=0)
    table_full = jnp.zeros((HEADS, grad_table_here.shape[1]), jnp.float32)
    table_full = lax.dynamic_update_slice_in_dim(
        table_full, grad_table_here, lax.axis_index("tensor") * heads_here, 0
    )
    total_gain_one, total_gain_two, total_router, total_table = lax.psum(
        (grad_gain_one, grad_gain_two, grad_router, table_full), ("dp", "tensor")
    )
    shard_rows = attn_gain.shape[0]
    dp_start = lax.axis_index("dp") * shard_rows
    grad_attn_gain = lax.dynamic_slice_in_dim(total_gain_one, dp_start, shard_rows, 0)
    grad_ffn_gain = lax.dynamic_slice_in_dim(total_gain_two, dp_start, shard_rows, 0)
    grad_router_mine = lax.dynamic_slice_in_dim(total_router, dp_start, shard_rows, 0)
    grad_table = lax.dynamic_slice_in_dim(
        total_table, lax.axis_index("tensor") * heads_here, heads_here, 0
    )
    return (
        layer_out,
        grad_tokens,
        grad_attn_gain,
        grad_ffn_gain,
        sum_query,
        sum_key,
        sum_value,
        sum_output,
        grad_table,
        grad_router_mine,
        sum_up,
        sum_down,
    )


def solution(mesh):
    in_specs = (
        P(("dp", "tensor"), None),
        P(("dp", "tensor"), None),
        P("dp", None),
        P(),
        P("dp"),
        P("dp"),
        P("dp", "tensor"),
        P("dp", "tensor"),
        P("dp", "tensor"),
        P("dp", "tensor"),
        P("tensor", None),
        P("dp", None),
        P(None, "dp", "tensor"),
        P(None, "dp", "tensor"),
    )
    out_specs = (
        P(("dp", "tensor"), None),
        P(("dp", "tensor"), None),
        P("dp"),
        P("dp"),
        P("dp", "tensor"),
        P("dp", "tensor"),
        P("dp", "tensor"),
        P("dp", "tensor"),
        P("tensor", None),
        P("dp", None),
        P(None, "dp", "tensor"),
        P(None, "dp", "tensor"),
    )
    return jax.shard_map(
        per_device, mesh=mesh, in_specs=in_specs, out_specs=out_specs, check_vma=False
    )
```

profile of v0, /device:TPU:0, one launch (start us, length us, event | category | flops | bytes accessed | tf_op | source)
XLA Modules:
  0.0 549.0 jit_solution(12500299910346789845)
XLA Ops:
  8.1 11.3 %all_gather.43 = bf16[768,192]{1,0:T(8,128)(2,1)S(1)} all-gather(bf16[96,192]{1,0:T(8,128)(2,1)} %param.22), channel_id=1, replica_groups=mesh['dp'=8,'tensor'=4] {'dp'}, dimensions={0}, use_global_device_ids=true | all-gather | bytes 331776 | tf_op jit(solution)/shard_map/all_gather | solution.py:102
  19.4 9.3 %all_gather.42 = bf16[768,192]{1,0:T(8,128)(2,1)S(1)} all-gather(bf16[96,192]{1,0:T(8,128)(2,1)} %param.21), channel_id=1, replica_groups=mesh['dp'=8,'tensor'=4] {'dp'}, dimensions={0}, use_global_device_ids=true | all-gather | bytes 331776 | tf_op jit(solution)/shard_map/all_gather | solution.py:101
  28.7 8.8 %all_gather.41 = bf16[768,192]{1,0:T(8,128)(2,1)S(1)} all-gather(bf16[96,192]{1,0:T(8,128)(2,1)} %param.20), channel_id=1, replica_groups=mesh['dp'=8,'tensor'=4] {'dp'}, dimensions={0}, use_global_device_ids=true | all-gather | bytes 331776 | tf_op jit(solution)/shard_map/all_gather | solution.py:100
  41.1 13.2 %all-reduce.6 = (bf16[768]{0:T(1024)(128)(2,1)S(1)}, bf16[768]{0:T(1024)(128)(2,1)S(1)}) all-reduce(bf16[768]{0:T(1024)(128)(2,1)S(1)} %dynamic-update-slice, bf16[768]{0:T(1024)(128)(2,1)S(1)} %dynamic-update-slice.1), channel_id=1, replica_groups=mesh['dp'=8,'tensor'=4] {'dp'}, use_global_device_ids=true, to_apply=%add.3 | all-reduce | flops 1536 | bytes 6144
  56.4 19.5 %all_gather.40 = bf16[512,768]{1,0:T(8,128)(2,1)S(1)} all-gather(bf16[128,768]{1,0:T(8,128)(2,1)S(1)} %fusion.17), channel_id=1, replica_groups=mesh['dp'=8,'tensor'=4] {'tensor'}, dimensions={0}, use_global_device_ids=true | all-gather | bytes 983040 | tf_op jit(solution)/shard_map/all_gather | solution.py:109
  81.5 7.1 %copy.81 = f32[1,3,512,1024]{3,1,2,0:T(4,128)S(1)} copy(f32[1,3,512,1024]{3,2,1,0:T(8,128)} %broadcast_bitcast_fusion) | data formatting | bytes 12582912
  88.6 6.3 %slice.53 = f32[3,523776]{1,0:T(4,128)} slice(f32[3,524288]{1,0:T(4,128)S(1)} %bitcast.97), slice={[0:3], [511:524287]} | slice | bytes 12570624 | tf_op jit(solution)/shard_map/slice | solution.py:50
  94.9 13.2 %reshape.172 = f32[3,512,1023]{2,1,0:T(8,128)} reshape(f32[3,523776]{1,0:T(4,128)} %slice.53) | data formatting | bytes 12570624 | tf_op jit(solution)/shard_map/reshape | solution.py:50
  116.0 9.3 %all_gather.44 = bf16[768,192]{1,0:T(8,128)(2,1)S(1)} all-gather(bf16[96,192]{1,0:T(8,128)(2,1)S(1)} %copy-done.32), channel_id=1, replica_groups=mesh['dp'=8,'tensor'=4] {'dp'}, dimensions={0}, use_global_device_ids=true | all-gather | bytes 331776 | tf_op jit(solution)/shard_map/all_gather | solution.py:103
  131.2 31.1 %reduce-scatter.15.cloned.1.call-done = f32[128,768]{1,0:T(8,128)} async-done(((f32[512,768]{1,0:T(8,128)}), f32[128,768]{1,0:T(8,128)}) %reduce-scatter.15.cloned.1.call-update) | async-done | bytes 393232 | tf_op jit(solution)/shard_map/reduce_scatter | solution.py:131
  163.6 18.2 %all_gather.47 = bf16[512,768]{1,0:T(8,128)(2,1)S(1)} all-gather(bf16[128,768]{1,0:T(8,128)(2,1)S(1)} %fusion.25), channel_id=1, replica_groups=mesh['dp'=8,'tensor'=4] {'tensor'}, dimensions={0}, use_global_device_ids=true | all-gather | bytes 983040 | tf_op jit(solution)/shard_map/all_gather | solution.py:153
  184.9 4.4 fusion.60
  189.4 19.2 %all-gather.6.cloned.1.call-done = bf16[4,768,768]{2,1,0:T(8,128)(2,1)} async-done(((bf16[4,96,768]{2,1,0:T(8,128)(2,1)}), bf16[4,768,768]{2,1,0:T(8,128)(2,1)}) %all-gather.6.cloned.1.call-update) | async-done | bytes 4718608 | tf_op jit(solution)/shard_map/all_gather | solution.py:164
  208.6 4.6 fusion.54
  215.8 9.0 %all-gather = bf16[8,96,4]{1,2,0:T(4,128)(2,1)S(1)} all-gather(bf16[1,96,4]{1,2,0:T(4,128)(2,1)S(1)} %bitcast.126), channel_id=1, replica_groups=mesh['dp'=8,'tensor'=4] {'dp'}, dimensions={0}, use_global_device_ids=true | all-gather | bytes 6912 | tf_op jit(solution)/shard_map/all_gather | solution.py:99
  225.4 25.8 %reduce-scatter.17.cloned.1.call-done = f32[128,768]{1,0:T(8,128)} async-done(((f32[512,768]{1,0:T(8,128)}), f32[128,768]{1,0:T(8,128)}) %reduce-scatter.17.cloned.1.call-update) | async-done | bytes 393232 | tf_op jit(solution)/shard_map/reduce_scatter | solution.py:171
  252.5 18.5 %all_gather.50 = bf16[512,768]{1,0:T(8,128)(2,1)} all-gather(bf16[128,768]{1,0:T(8,128)(2,1)S(1)} %fusion.19), channel_id=1, replica_groups=mesh['dp'=8,'tensor'=4] {'tensor'}, dimensions={0}, use_global_device_ids=true | all-gather | bytes 983040 | tf_op jit(solution)/shard_map/all_gather | solution.py:176
  289.5 5.8 %copy.62 = bf16[4,768,768]{2,0,1:T(4,128)(2,1)} copy(bf16[4,768,768]{2,1,0:T(8,128)(2,1)S(1)} %convolution_convert_fusion.1) | data formatting | bytes 9437184 | tf_op jit(solution)/shard_map/convert_element_type | solution.py:267
  295.3 4.6 all-to-all-start
  300.0 21.2 %reduce-scatter.19.cloned.1.call-done = f32[128,768]{1,0:T(8,128)} async-done(((f32[512,768]{1,0:T(8,128)}), f32[128,768]{1,0:T(8,128)}) %reduce-scatter.19.cloned.1.call-update) | async-done | bytes 393232 | tf_op jit(solution)/shard_map/reduce_scatter | solution.py:194
  323.6 18.3 %all_gather.51 = bf16[512,768]{1,0:T(8,128)(2,1)S(1)} all-gather(bf16[128,768]{1,0:T(8,128)(2,1)S(1)} %fusion.53), channel_id=1, replica_groups=mesh['dp'=8,'tensor'=4] {'tensor'}, dimensions={0}, use_global_device_ids=true | all-gather | bytes 983040 | tf_op jit(solution)/shard_map/all_gather | solution.py:199
  360.1 5.7 %copy.63 = bf16[4,768,768]{2,0,1:T(4,128)(2,1)} copy(bf16[4,768,768]{2,1,0:T(8,128)(2,1)S(1)} %convolution_convert_fusion) | data formatting | bytes 9437184 | tf_op jit(solution)/shard_map/convert_element_type | solution.py:270
  369.7 4.7 copy.83
  375.6 4.6 all-to-all-start.1
  380.5 7.1 %pad_convert_fusion = f32[3,524800]{1,0:T(4,128)} fusion(bf16[3,524288]{1,0:T(4,128)(2,1)} %bitcast.98), kind=kLoop, calls=%fused_computation.6 | loop fusion | flops 1574400 | bytes 9443328 | tf_op jit(solution)/shard_map/reshape | solution.py:68
  387.6 14.8 %reshape.187 = f32[3,512,1025]{2,1,0:T(8,128)} reshape(f32[3,524800]{1,0:T(4,128)} %pad_convert_fusion) | data formatting | bytes 12595200 | tf_op jit(solution)/shard_map/reshape | solution.py:68
  407.9 4.7 convert_reduce_fusion.1
  412.6 25.5 %all-to-all-done.1 = bf16[4,768,768]{2,0,1:T(4,128)(2,1)} async-done(((bf16[4,768,768]{2,0,1:T(4,128)(2,1)}), bf16[4,768,768]{2,0,1:T(4,128)(2,1)}, u32[]{:S(2)}, u32[]{:S(2)}) %all-to-all-start.1) | async-done | bytes 4718624 | tf_op jit(solution)/shard_map/all_to_all | solution.py:269
  438.1 4.8 convert_reduce_fusion
  446.4 38.2 %all-reduce.5 = (f32[768]{0:T(1024)S(1)}, f32[768]{0:T(1024)S(1)}, f32[12,32]{1,0:T(8,128)S(1)}, f32[768,4]{0,1:T(4,128)S(1)}) all-reduce(f32[768]{0:T(1024)S(1)} %get-tuple-element.62, f32[768]{0:T(1024)S(1)} %get-tuple-element.60, f32[12,32]{1,0:T(8,128)S(1)} %dynamic_update_slice.3, ...), channel_id=1, replica_groups=mesh['dp'=8,'tensor'=4] {'dp','tensor'}, use_global_device_ids=true, to_apply=%region_22.23 | all-reduce | flops 4992 | bytes 39936 | tf_op jit(solution)/shard_map/psum | solution.py:279
  489.1 13.4 %reduce-scatter.29.cloned.1.call-done = f32[96,192]{1,0:T(8,128)} async-done(((f32[768,192]{1,0:T(8,128)}), f32[96,192]{1,0:T(8,128)}) %reduce-scatter.29.cloned.1.call-update) | async-done | bytes 73744
  502.5 38.7 %reduce-scatter.23.cloned.1.call-done = f32[96,192]{1,0:T(8,128)} async-done(((f32[768,192]{1,0:T(8,128)}), f32[96,192]{1,0:T(8,128)}) %reduce-scatter.23.cloned.1.call-update) | async-done | bytes 73744 | tf_op jit(solution)/shard_map/reduce_scatter | solution.py:260
  (187 shorter events, 90.9 us)
Async XLA Ops:
  8.0 69.7 %copy-start = (bf16[3,32]{1,0:T(4,128)(2,1)S(1)}, bf16[3,32]{1,0:T(4,128)(2,1)}, u32[]{:S(2)}) copy-start(bf16[3,32]{1,0:T(4,128)(2,1)} %param.24) | copy-start | bytes 580
  8.0 154.3 %reduce-scatter.15.cloned.1.call-start = ((), (), s32[]{:S(2)}) async-start(), calls=%async_computation.10 | async-start | bytes 1966080 | tf_op jit(solution)/shard_map/reduce_scatter | solution.py:131
  19.4 57.6 %copy-start.23 = (bf16[768,192]{1,0:T(8,128)(2,1)}, bf16[768,192]{1,0:T(8,128)(2,1)S(1)}, u32[]{:S(2)}) copy-start(bf16[768,192]{1,0:T(8,128)(2,1)S(1)} %all_gather.43) | copy-start | bytes 884740
  28.7 48.3 %copy-start.25 = (bf16[768,192]{1,0:T(8,128)(2,1)}, bf16[768,192]{1,0:T(8,128)(2,1)S(1)}, u32[]{:S(2)}) copy-start(bf16[768,192]{1,0:T(8,128)(2,1)S(1)} %all_gather.42) | copy-start | bytes 884740
  37.5 39.4 %copy-start.27 = (bf16[768,192]{1,0:T(8,128)(2,1)}, bf16[768,192]{1,0:T(8,128)(2,1)S(1)}, u32[]{:S(2)}) copy-start(bf16[768,192]{1,0:T(8,128)(2,1)S(1)} %all_gather.41) | copy-start | bytes 884740
  55.4 21.6 %copy-start.35 = (f32[128]{0:T(128)}, f32[128]{0:T(128)S(1)}, u32[]{:S(2)}) copy-start(f32[128]{0:T(128)S(1)} %fusion.22) | copy-start | bytes 1540
  77.7 34.8 %copy-start.18 = (bf16[512,192]{0,1:T(8,128)(2,1)}, bf16[512,192]{0,1:T(8,128)(2,1)S(1)}, u32[]{:S(2)}) copy-start(bf16[512,192]{0,1:T(8,128)(2,1)S(1)} %get-tuple-element.77) | copy-start | bytes 589828
  77.7 47.6 %copy-start.14 = (bf16[512,192]{0,1:T(8,128)(2,1)}, bf16[512,192]{0,1:T(8,128)(2,1)S(1)}, u32[]{:S(2)}) copy-start(bf16[512,192]{0,1:T(8,128)(2,1)S(1)} %get-tuple-element.79) | copy-start | bytes 589828
  115.1 10.2 %copy-start.2 = (f32[3,512,512]{1,2,0:T(8,128)}, f32[3,512,512]{1,2,0:T(8,128)S(1)}, u32[]{:S(2)}) copy-start(f32[3,512,512]{1,2,0:T(8,128)S(1)} %get-tuple-element.83) | copy-start | bytes 9437188
  128.2 34.2 %copy-start.4 = (bf16[128,768]{1,0:T(8,128)(2,1)S(1)}, bf16[128,768]{1,0:T(8,128)(2,1)}, u32[]{:S(2)}) copy-start(bf16[128,768]{1,0:T(8,128)(2,1)} %param.14) | copy-start | bytes 589828
  128.2 56.7 %all-gather.4.cloned.1.call-start = ((), (), s32[]{:S(2)}) async-start(), calls=%async_computation.11 | async-start | bytes 5308416 | tf_op jit(solution)/shard_map/all_gather | solution.py:163
  128.8 79.8 %all-gather.6.cloned.1.call-start = ((), (), s32[]{:S(2)}) async-start(), calls=%async_computation.12 | async-start | bytes 5308416 | tf_op jit(solution)/shard_map/all_gather | solution.py:164
  129.4 121.8 %reduce-scatter.17.cloned.1.call-start = ((), (), s32[]{:S(2)}) async-start(), calls=%async_computation.13 | async-start | bytes 1966080 | tf_op jit(solution)/shard_map/reduce_scatter | solution.py:171
  215.7 35.5 %copy-start.12 = (bf16[128,768]{1,0:T(8,128)(2,1)S(1)}, bf16[128,768]{1,0:T(8,128)(2,1)}, u32[]{:S(2)}) copy-start(bf16[128,768]{1,0:T(8,128)(2,1)} %param.15) | copy-start | bytes 589828
  215.8 59.4 %copy-start.5 = (f32[4,144,768]{2,1,0:T(8,128)S(1)}, f32[4,144,768]{2,1,0:T(8,128)}, u32[]{:S(2)}) copy-start(f32[4,144,768]{2,1,0:T(8,128)} %fusion.60) | copy-start | bytes 5308420
  215.8 105.4 %reduce-scatter.19.cloned.1.call-start = ((), (), s32[]{:S(2)}) async-start(), calls=%async_computation.14 | async-start | bytes 1966080 | tf_op jit(solution)/shard_map/reduce_scatter | solution.py:194
  279.4 4.4 copy-start.6
  295.3 80.3 %all-to-all-start = ((bf16[4,768,768]{2,0,1:T(4,128)(2,1)}), bf16[4,768,768]{2,0,1:T(4,128)(2,1)}, u32[]{:S(2)}, u32[]{:S(2)}) async-start(bf16[4,768,768]{2,0,1:T(4,128)(2,1)} %copy.62), calls=%async_computation.5 | async-start | bytes 9437184 | tf_op jit(solution)/shard_map/all_to_all | solution.py:266
  299.9 42.0 %copy-start.11 = (bf16[768,192]{1,0:T(8,128)(2,1)S(1)}, bf16[768,192]{1,0:T(8,128)(2,1)}, u32[]{:S(2)}) copy-start(bf16[768,192]{1,0:T(8,128)(2,1)} %copy-done.10) | copy-start | bytes 884740
  299.9 145.4 %reduce-scatter.21.cloned.1.call-start = ((), (), s32[]{:S(2)}) async-start(), calls=%async_computation.15 | async-start | bytes 983040 | tf_op jit(solution)/shard_map/reduce_scatter | solution.py:244
  323.5 18.8 %copy-start.3 = (f32[3,512,512]{1,2,0:T(8,128)S(1)}, f32[3,512,512]{1,2,0:T(8,128)}, u32[]{:S(2)}) copy-start(f32[3,512,512]{1,2,0:T(8,128)} %copy-done.2) | copy-start | bytes 9437188
  323.5 18.9 %copy-start.15 = (bf16[512,192]{0,1:T(8,128)(2,1)S(1)}, bf16[512,192]{0,1:T(8,128)(2,1)}, u32[]{:S(2)}) copy-start(bf16[512,192]{0,1:T(8,128)(2,1)} %copy-done.14) | copy-start | bytes 589828
  348.7 140.4 %reduce-scatter.25.cloned.1.call-start = ((), (), s32[]{:S(2)}) async-start(), calls=%async_computation.17 | async-start | bytes 884736
  354.3 134.8 %reduce-scatter.27.cloned.1.call-start = ((), (), s32[]{:S(2)}) async-start(), calls=%async_computation.18 | async-start | bytes 884736
  356.6 145.9 %reduce-scatter.29.cloned.1.call-start = ((), (), s32[]{:S(2)}) async-start(), calls=%async_computation.19 | async-start | bytes 884736
  369.7 4.7 copy-start.13
  375.6 62.5 %all-to-all-start.1 = ((bf16[4,768,768]{2,0,1:T(4,128)(2,1)}), bf16[4,768,768]{2,0,1:T(4,128)(2,1)}, u32[]{:S(2)}, u32[]{:S(2)}) async-start(bf16[4,768,768]{2,0,1:T(4,128)(2,1)} %copy.63), calls=%async_computation.6 | async-start | bytes 9437184 | tf_op jit(solution)/shard_map/all_to_all | solution.py:269
  380.2 161.0 %reduce-scatter.23.cloned.1.call-start = ((), (), s32[]{:S(2)}) async-start(), calls=%async_computation.16 | async-start | bytes 884736 | tf_op jit(solution)/shard_map/reduce_scatter | solution.py:260
  444.1 43.0 %copy-start.36 = (f32[128]{0:T(128)S(1)}, f32[128]{0:T(128)}, u32[]{:S(2)}) copy-start(f32[128]{0:T(128)} %copy-done.35) | copy-start | bytes 1540
  444.1 43.0 %copy-start.9 = (f32[128,768]{1,0:T(8,128)S(1)}, f32[128,768]{1,0:T(8,128)}, u32[]{:S(2)}) copy-start(f32[128,768]{1,0:T(8,128)} %copy-done.8) | copy-start | bytes 1179652
  444.1 43.0 %copy-start.21 = (f32[128,768]{1,0:T(8,128)S(1)}, f32[128,768]{1,0:T(8,128)}, u32[]{:S(2)}) copy-start(f32[128,768]{1,0:T(8,128)} %reduce-scatter.17.cloned.1.call-done) | copy-start | bytes 1179652
  444.1 97.2 %copy-start.1 = (bf16[3,32]{1,0:T(4,128)(2,1)S(1)}, bf16[3,32]{1,0:T(4,128)(2,1)}, u32[]{:S(2)}) copy-start(bf16[3,32]{1,0:T(4,128)(2,1)} %param.24) | copy-start | bytes 580
  (20 other events, 25.9 us)
Sparse Core Ops, SparseCore 0:
  128.3 33.9 reduce-scatter.14
  215.9 35.2 reduce-scatter.16
  287.0 34.1 reduce-scatter.18
  348.8 22.6 reduce-scatter.20
  375.1 47.8 reduce-scatter.24
  426.5 37.2 reduce-scatter.26
  467.5 34.9 reduce-scatter.28
  506.2 34.9 reduce-scatter.22
Sparse Core Ops, SparseCore 1:
  130.6 37.4 all-gather.3
  169.8 38.7 all-gather.5
where the time goes:
time: 558 us; the launch traced here: 549 us
  waiting for transfers between devices  176 us (32%)
  blocking collectives  173 us (31%)
  local copies, waits for them, and re-layouts  102 us (18%)
  matrix products  39.3 us (7%)
  other arithmetic  30.9 us (6%)
  between operations  17.1 us (3%)
  starting transfers between devices  10.1 us (2%)
    reduce_scatter x1, waiting for transfers between devices, per_device(): lax.psum_scatter(grad_output, 'dp', scatter_dimension=0, tiled=True)  38.7 us
    psum x1, blocking collectives, per_device(): lax.psum((grad_gain_one, grad_gain_two, grad_router, table_full), ('dp',...  38.2 us
    unnamed x95, local copies, waits for them, and re-layouts  36.2 us
    reduce_scatter x1, waiting for transfers between devices, per_device(): lax.psum_scatter(lax.dot_general(selected, output_full, (((1,), (1,)), ((...  31.1 us
    reduce_scatter x1, waiting for transfers between devices, per_device(): lax.psum_scatter(expert_rows[targets], 'tensor', scatter_dimension=0, til...  25.8 us
    all_to_all x1, waiting for transfers between devices, per_device(): lax.all_to_all(grad_down.astype(jnp.bfloat16), 'dp', split_axis=1, concat...  25.5 us
    reduce_scatter x1, waiting for transfers between devices, per_device(): lax.psum_scatter(grad_disp[targets], 'tensor', scatter_dimension=0, tiled...  21.2 us
    all_gather x1, blocking collectives, per_device(): lax.all_gather(normed_one.astype(jnp.bfloat16), 'tensor', axis=0, tiled=T...  19.5 us
  transfers between devices with their start and end apart: 12, of which 7 were waited for; matrix products, arithmetic and copies ran while one was open for 18% of the time, Pallas kernels for 0%

commit v1 on v0

v1 whole, which is shorter than its diff:
```python
import math

import jax
import jax.numpy as jnp
from jax import lax
from jax.experimental import pallas as pl
from jax.experimental.pallas import tpu as pltpu
from jax.sharding import PartitionSpec as P

CAP = 144
EPS = 1e-06
HIGHEST = lax.Precision.HIGHEST
BF = jnp.bfloat16
F32 = jnp.float32
SMALL = 128
GELU_A = math.sqrt(2 / math.pi)
GELU_B = 0.044715


def dot(a, b, ca=1, cb=0, precision=None):
    return lax.dot_general(
        a, b, (((ca,), (cb,)), ((), ())), precision=precision, preferred_element_type=F32
    )


def call(kernel, outs, cost, **kw):
    return pl.pallas_call(
        kernel,
        out_shape=outs,
        compiler_params=pltpu.CompilerParams(vmem_limit_bytes=56 * 1024 * 1024),
        cost_estimate=pl.CostEstimate(flops=cost, bytes_accessed=12_000_000, transcendentals=0),
        **kw,
    )


def head_mask(shape, head, size):
    lane = lax.broadcasted_iota(jnp.int32, shape, 1)
    return (lane >= head * size) & (lane < (head + 1) * size)


def bucket_hot(buckets, count):
    ids = lax.broadcasted_iota(jnp.int32, (count, buckets.shape[1]), 0)
    return ids == buckets


def attention_forward(heads, size, tok, gain, wqkv, wout, table, buckets, na, qkv, probs, ctx, part):
    length = tok.shape[0]
    wide = 2 * length
    width = heads * size
    x = tok[...].astype(F32)
    r1 = lax.rsqrt(jnp.mean(x * x, axis=-1, keepdims=True) + EPS)
    rows = (x * r1 * gain[...]).astype(BF)
    na[...] = rows
    proj = dot(rows, wqkv[...]).astype(BF)
    qkv[...] = proj
    q, k, v = qkv[:, :width], qkv[:, width : 2 * width], qkv[:, 2 * width :]
    hot = bucket_hot(buckets[...], table.shape[1]).astype(F32).astype(BF)
    rel = dot(table[...], hot)
    row8 = lax.broadcasted_iota(jnp.int32, (8, wide), 0)
    total = jnp.zeros((length, width), F32)
    for h in range(heads):
        bias = jnp.broadcast_to(rel[h : h + 1, :], (8, wide))
        bias = pltpu.roll(bias, wide - (length - 1), 1)
        for bit in (1, 2, 4):
            bias = jnp.where((row8 & bit) != 0, pltpu.roll(bias, bit, 1), bias)
        step = 8
        while step < length:
            bias = jnp.concatenate([bias, pltpu.roll(bias, step, 1)], axis=0)
            step *= 2
        mask = head_mask(q.shape, h, size)
        scores = dot(jnp.where(mask, q, jnp.zeros_like(q)), k, 1, 1) + bias[:, :length]
        peak = jnp.max(scores, axis=-1, keepdims=True)
        ex = jnp.exp(scores - peak)
        p = ex / jnp.sum(ex, axis=-1, keepdims=True)
        probs[h] = p
        total = total + jnp.where(mask, dot(p.astype(BF), v), 0.0)
    c = total.astype(BF)
    ctx[...] = c
    part[...] = dot(c, wout[...], 1, 1).astype(BF)


def attention_backward(
    heads, size, tok, na, qkv, probs, ctx, gh, wqkv, wout, gain, buckets, gw, gout, gna, gain_grad, gtable
):
    length = tok.shape[0]
    wide = 2 * length
    width = heads * size
    q, k, v = qkv[:, :width], qkv[:, width : 2 * width], qkv[:, 2 * width :]
    g = gh[...]
    gout[...] = dot(g, ctx[...], 0, 0).astype(BF)
    gctx = dot(g, wout[...]).astype(BF)
    zero = jnp.zeros((length, width), F32)
    gq, gk, gv = zero, zero, zero
    row8 = lax.broadcasted_iota(jnp.int32, (8, wide), 0)
    diag = jnp.zeros((8, wide), F32)
    for h in range(heads):
        mask = head_mask(q.shape, h, size)
        p = probs[h]
        pb = p.astype(BF)
        dp = dot(jnp.where(mask, gctx, jnp.zeros_like(gctx)), v, 1, 1)
        inner = jnp.sum(p * dp, axis=-1, keepdims=True)
        gs = (p * (dp - inner)).astype(BF)
        gq = gq + jnp.where(mask, dot(gs, k), 0.0)
        gk = gk + jnp.where(mask, dot(gs, q, 0, 0), 0.0)
        gv = gv + jnp.where(mask, dot(pb, gctx, 0, 0), 0.0)
        t = jnp.concatenate([gs.astype(F32), jnp.zeros((length, wide - length), F32)], axis=1)
        half = length // 2
        while half >= 8:
            t = t[:half] + pltpu.roll(t[half:], wide - half, 1)
            half //= 2
        for bit in (1, 2, 4):
            t = jnp.where((row8 & bit) != 0, pltpu.roll(t, wide - bit, 1), t)
        t = jnp.sum(t, axis=0, keepdims=True)
        t = pltpu.roll(jnp.broadcast_to(t, (8, wide)), length - 1, 1)
        diag = jnp.where(row8 == h, t, diag)
    hot = bucket_hot(buckets[...], gtable.shape[1]).astype(F32)
    gtable[...] = dot(diag, hot, 1, 1, HIGHEST)
    gq, gk, gv = gq.astype(BF), gk.astype(BF), gv.astype(BF)
    rows = na[...]
    grad_na = jnp.zeros((length, tok.shape[1]), F32)
    for i, part in enumerate((gq, gk, gv)):
        gw[i] = dot(rows, part, 0, 0).astype(BF)
        grad_na = grad_na + dot(part, wqkv[:, i * width : (i + 1) * width], 1, 1)
    gna[...] = grad_na.astype(BF)
    x = tok[...].astype(F32)
    r1 = lax.rsqrt(jnp.mean(x * x, axis=-1, keepdims=True) + EPS)
    gain_grad[...] = jnp.sum(grad_na * (x * r1), axis=0, keepdims=True)


def ffn_kernel(cap, routes, rows, gating, cot, up, down, ret, gnf, gup, gdown, gret):
    e = pl.program_id(0)
    length, model = rows.shape

    @pl.when(e == 0)
    def _():
        ret[...] = jnp.zeros_like(ret)
        gnf[...] = jnp.zeros_like(gnf)
        gret[...] = (gating[...] * cot[...].astype(F32)).astype(BF)

    match = jnp.broadcast_to(routes[...] == e, (8, length))
    a = lax.broadcasted_iota(jnp.int32, (length, length), 0)
    b = lax.broadcasted_iota(jnp.int32, (length, length), 1)
    before = jnp.where(a < b, 1.0, 0.0).astype(BF)
    slot = dot(jnp.where(match, 1.0, 0.0).astype(BF), before)
    slot = jnp.where(match, slot, -1.0)[0:1, :].astype(jnp.int32)
    place = jnp.where(
        lax.broadcasted_iota(jnp.int32, (cap, length), 0) == slot, 1.0, 0.0
    ).astype(BF)
    upw, downw = up[0], down[0]
    disp = dot(place, rows[...]).astype(BF)
    gslot = dot(place, gret[...]).astype(BF)
    pre = dot(disp, upw)
    th = jnp.tanh(GELU_A * (pre + GELU_B * pre * pre * pre))
    act = (0.5 * pre * (1.0 + th)).astype(BF)
    slope = 0.5 * (1.0 + th) + 0.5 * pre * (1.0 - th * th) * GELU_A * (
        1.0 + 3.0 * GELU_B * pre * pre
    )
    gpre = (slope * dot(gslot, downw)).astype(BF)
    gdown[0] = dot(gslot, act, 0, 0).astype(BF)
    gup[0] = dot(disp, gpre, 0, 0).astype(BF)
    out = dot(act, downw, 1, 1).astype(BF)
    ret[...] += dot(place, out, 0, 0).astype(BF)
    back = dot(gpre, upw, 1, 1).astype(BF)
    gnf[...] += dot(place, back, 0, 0).astype(BF)


def per_device(
    tokens,
    cotangent,
    routes,
    buckets,
    attn_gain,
    ffn_gain,
    w_query,
    w_key,
    w_value,
    w_output,
    rel_table,
    w_router,
    expert_up,
    expert_down,
):
    local_rows, model = tokens.shape
    length = local_rows * lax.axis_size("tensor")
    heads = rel_table.shape[0]
    width = w_query.shape[1]
    size = width // heads
    experts = expert_up.shape[0]
    shard = attn_gain.shape[0]
    count = rel_table.shape[1]
    hidden_here = expert_up.shape[2]

    up_full = lax.all_gather(expert_up, "dp", axis=1, tiled=True)
    down_full = lax.all_gather(expert_down, "dp", axis=1, tiled=True)
    small = jnp.concatenate([attn_gain[:, None], ffn_gain[:, None], w_router], axis=1)
    small = jnp.pad(small, ((0, 0), (0, SMALL - small.shape[1])))
    pack = jnp.concatenate([w_query, w_key, w_value, w_output, small], axis=1)
    pack = lax.all_gather(pack, "dp", axis=0, tiled=True)
    both = lax.all_gather(
        jnp.concatenate([tokens, cotangent], axis=1), "tensor", axis=0, tiled=True
    )
    tok_all, cot_all = both[:, :model], both[:, model:]
    wqkv, wout = pack[:, : 3 * width], pack[:, 3 * width : 4 * width]
    small = pack[:, 4 * width :].astype(F32)
    gain_one = small[:, 0].reshape(1, model)
    gain_two = small[:, 1].reshape(1, model)
    router = small[:, 2 : 2 + experts]
    bucket_row = jnp.pad(buckets, (0, 2 * length - buckets.shape[0]), constant_values=-1)[None, :]
    table8 = jnp.pad(rel_table, ((0, 16 - heads), (0, 0)))

    def sds(shape, dtype=BF):
        return jax.ShapeDtypeStruct(shape, dtype)

    na, qkv, probs, ctx, part = call(
        lambda *refs: attention_forward(heads, size, *refs),
        (
            sds((length, model)),
            sds((length, 3 * width)),
            sds((heads, length, length), F32),
            sds((length, width)),
            sds((length, model)),
        ),
        3_000_000_000,
        name="attention_forward",
    )(tok_all, gain_one, wqkv, wout, table8, bucket_row)
    attended = lax.psum_scatter(part, "tensor", scatter_dimension=0, tiled=True)

    token_rows = tokens.astype(F32)
    hidden = token_rows + attended.astype(F32)
    route_all = routes[:, 0]
    route_mine = lax.dynamic_slice_in_dim(
        route_all, lax.axis_index("tensor") * local_rows, local_rows
    )
    chosen = (route_mine[:, None] == jnp.arange(experts, dtype=jnp.int32)[None, :]).astype(F32)
    r2 = lax.rsqrt(jnp.mean(hidden * hidden, axis=-1, keepdims=True) + EPS)
    u2 = hidden * r2
    nf = u2 * gain_two
    prob = jax.nn.softmax(jnp.dot(nf, router, precision=HIGHEST), axis=-1)
    gating = jnp.sum(prob * chosen, axis=-1, keepdims=True)
    gate_high = gating.astype(BF)
    gate_low = (gating - gate_high.astype(F32)).astype(BF)
    gate_cols = jnp.pad(jnp.concatenate([gate_high, gate_low], axis=1), ((0, 0), (0, SMALL - 2)))
    nf_all = lax.all_gather(
        jnp.concatenate([nf.astype(BF), gate_cols], axis=1), "tensor", axis=0, tiled=True
    )
    gate_all = jnp.sum(nf_all[:, model : model + 2].astype(F32), axis=1, keepdims=True)

    whole = lambda *shape: pl.BlockSpec(shape, lambda e: (0,) * len(shape))
    per_expert = pl.BlockSpec((1, model, hidden_here), lambda e: (e, 0, 0))
    ret, gnf, grad_up, grad_down = call(
        lambda *refs: ffn_kernel(CAP, *refs),
        (
            sds((length, model)),
            sds((length, model)),
            sds((experts, model, hidden_here)),
            sds((experts, model, hidden_here)),
        ),
        6_000_000_000,
        name="experts",
        grid=(experts,),
        in_specs=[
            whole(1, length),
            whole(length, model),
            whole(length, 1),
            whole(length, model),
            per_expert,
            per_expert,
        ],
        out_specs=[whole(length, model), whole(length, model), per_expert, per_expert],
        scratch_shapes=[pltpu.VMEM((length, model), BF)],
    )(route_all[None, :], nf_all[:, :model], gate_all, cot_all, up_full, down_full)

    traded_up = lax.all_to_all(grad_up, "dp", split_axis=1, concat_axis=0, tiled=True)
    traded_down = lax.all_to_all(grad_down, "dp", split_axis=1, concat_axis=0, tiled=True)

    summed = lax.psum_scatter(
        jnp.concatenate([ret, gnf], axis=1), "tensor", scatter_dimension=0, tiled=True
    ).astype(F32)
    returned, grad_nf = summed[:, :model], summed[:, model:]
    layer_out = (hidden + gating * returned).astype(BF)
    g = cotangent.astype(F32)
    grad_gating = jnp.sum(g * returned, axis=-1, keepdims=True)
    grad_logits = prob * (chosen - gating) * grad_gating
    grad_router = lax.dot_general(
        nf, grad_logits, (((0,), (0,)), ((), ())), precision=HIGHEST, preferred_element_type=F32
    )
    grad_n2 = grad_nf + lax.dot_general(
        grad_logits, router, (((1,), (1,)), ((), ())), precision=HIGHEST, preferred_element_type=F32
    )
    gn2 = grad_n2 * gain_two
    grad_gain_two = jnp.sum(grad_n2 * u2, axis=0)
    grad_hidden = g + r2 * (gn2 - u2 * jnp.mean(gn2 * u2, axis=-1, keepdims=True))
    gh_all = lax.all_gather(grad_hidden.astype(BF), "tensor", axis=0, tiled=True)

    gw, gout, gna, grad_gain_one, gtable = call(
        lambda *refs: attention_backward(heads, size, *refs),
        (
            sds((3, model, width)),
            sds((model, width)),
            sds((length, model)),
            sds((1, model), F32),
            sds((8, count), F32),
        ),
        4_000_000_000,
        name="attention_backward",
    )(tok_all, na, qkv, probs, ctx, gh_all, wqkv, wout, gain_one, bucket_row)
    grad_na = lax.psum_scatter(gna, "tensor", scatter_dimension=0, tiled=True).astype(F32)
    r1 = lax.rsqrt(jnp.mean(token_rows * token_rows, axis=-1, keepdims=True) + EPS)
    u1 = token_rows * r1
    gn1 = grad_na * gain_one
    grad_tokens = grad_hidden + r1 * (gn1 - u1 * jnp.mean(gn1 * u1, axis=-1, keepdims=True))

    flat_table = jnp.broadcast_to(gtable[:heads].reshape(1, heads * count), (model, heads * count))
    cols = jnp.concatenate(
        [grad_gain_one.reshape(model, 1), grad_gain_two[:, None], grad_router, flat_table], axis=1
    )
    cols = jnp.pad(cols, ((0, 0), (0, SMALL - cols.shape[1]))).astype(BF)
    summed = lax.psum_scatter(
        jnp.concatenate([gw[0], gw[1], gw[2], gout, cols], axis=1),
        "dp",
        scatter_dimension=0,
        tiled=True,
    ).astype(F32)
    grads = [summed[:, i * width : (i + 1) * width] for i in range(4)]
    smalls = summed[:, 4 * width :]
    start = 2 + experts
    grad_table = smalls[0, start : start + heads * count].reshape(heads, count)
    total = lax.psum(smalls[:, :start], "tensor")

    owners = lax.axis_size("dp")
    sum_up = jnp.sum(
        traded_up.reshape(owners, experts, shard, hidden_here).astype(F32), axis=0
    )
    sum_down = jnp.sum(
        traded_down.reshape(owners, experts, shard, hidden_here).astype(F32), axis=0
    )
    return (
        layer_out,
        grad_tokens,
        total[:, 0],
        total[:, 1],
        *grads,
        grad_table,
        total[:, 2:start],
        sum_up,
        sum_down,
    )


def solution(mesh):
    rows = P(("dp", "tensor"), None)
    square = P("dp", "tensor")
    expert = P(None, "dp", "tensor")
    in_specs = (
        rows, rows, P("dp", None), P(), P("dp"), P("dp"), square, square, square, square,
        P("tensor", None), P("dp", None), expert, expert,
    )
    out_specs = (
        rows, rows, P("dp"), P("dp"), square, square, square, square,
        P("tensor", None), P("dp", None), expert, expert,
    )
    return jax.shard_map(
        per_device, mesh=mesh, in_specs=in_specs, out_specs=out_specs, check_vma=False
    )
```

time: 558 us -> 406 us (0.73); the launches traced: 549 us -> 405 us
  blocking collectives: 173 us -> 59.1 us
  local copies, waits for them, and re-layouts: 102 us -> 39.2 us
  waiting for transfers between devices: 176 us -> 225 us
  matrix products: 39.3 us -> 2.54 us
  Pallas kernels: 0 us -> 31.1 us
  other arithmetic: 30.9 us -> 23.5 us
    all_gather x2 -> x4, waiting for transfers between devices: 19.2 us -> 115 us  [the longest x1 40.7 us: per_device(): down_full = lax.all_gather(expert_down, 'dp', axis=1, tiled=True)]
    all_gather x9 -> x2, blocking collectives: 122 us -> 39.6 us  [the longest x1 20 us: per_device(): lax.all_gather(grad_hidden.astype(BF), 'tensor', axis=0, tiled=True)]
    dot_general x23 -> x3, matrix products: 39.3 us -> 2.54 us  [the longest x1 1.47 us: per_device(): prob = jax.nn.softmax(jnp.dot(nf, router, precision=HIGHEST), axis=-1)]
    reduce_scatter x5 -> x4, waiting for transfers between devices: 117 us -> 82.9 us  [the longest x1 31.4 us: per_device(): lax.psum_scatter(jnp.concatenate([gw[0], gw[1], gw[2], gout, cols], axis=...]
    unnamed x95 -> x31, local copies, waits for them, and re-layouts: 36.2 us -> 4.16 us
    pallas_call x0 -> x3, Pallas kernels: none -> 31.1 us  [the longest x1 15 us: per_device(): call(lambda *refs: ffn_kernel(CAP, *refs), (sds((length, model)), sds((le...]
    reshape x2 -> x1, local copies, waits for them, and re-layouts: 28 us -> 0.19 us  [per_device(): grad_gain_one.reshape(model, 1)]
    psum x1, blocking collectives: 38.2 us -> 19.5 us  [per_device(): total = lax.psum(smalls[:, :start], 'tensor')]
  transfers between devices with their start and end apart: 12 -> 10, of which waited for: 7 -> 9; matrix products, arithmetic and copies ran while one was open for 18% -> 11% of each run, Pallas kernels for 0% -> 2%
where the time goes in v1:
time: 406 us; the launch traced here: 405 us
  waiting for transfers between devices  225 us (55%)
  blocking collectives  59.1 us (15%)
  local copies, waits for them, and re-layouts  39.2 us (10%)
  Pallas kernels  31.1 us (8%)
  other arithmetic  23.5 us (6%)
  between operations  14.4 us (4%)
  starting transfers between devices  9.89 us (2%)
    all_gather x1, waiting for transfers between devices, per_device(): down_full = lax.all_gather(expert_down, 'dp', axis=1, tiled=True)  40.7 us
    all_gather x1, waiting for transfers between devices, per_device(): lax.all_gather(jnp.concatenate([tokens, cotangent], axis=1), 'tensor', ax...  37.1 us
    reduce_scatter x1, waiting for transfers between devices, per_device(): lax.psum_scatter(jnp.concatenate([gw[0], gw[1], gw[2], gout, cols], axis=...  31.4 us
    reduce_scatter x1, waiting for transfers between devices, per_device(): lax.psum_scatter(jnp.concatenate([ret, gnf], axis=1), 'tensor', scatter_d...  29.9 us
    all_gather x1, waiting for transfers between devices, per_device(): pack = lax.all_gather(pack, 'dp', axis=0, tiled=True)  23.6 us
    reduce_scatter x1, waiting for transfers between devices, per_device(): attended = lax.psum_scatter(part, 'tensor', scatter_dimension=0, tiled=True)  21.6 us
    all_gather x1, blocking collectives, per_device(): lax.all_gather(grad_hidden.astype(BF), 'tensor', axis=0, tiled=True)  20 us
    all_gather x1, blocking collectives, per_device(): lax.all_gather(jnp.concatenate([nf.astype(BF), gate_cols], axis=1), 'tens...  19.6 us
  transfers between devices with their start and end apart: 10, of which 9 were waited for; matrix products, arithmetic and copies ran while one was open for 11% of the time, Pallas kernels for 2%

profile of v1, /device:TPU:0, one launch (start us, length us, event | category | flops | bytes accessed | tf_op | source)
XLA Modules:
  0.0 405.2 jit_solution(10980850577298490712)
XLA Ops:
  7.2 1.8 pad_maximum_fusion.1
  10.0 1.7 concatenate.27
  12.9 37.1 %all-gather.5.cloned.1.call-done = bf16[512,1536]{1,0:T(8,128)(2,1)} async-done(((bf16[128,1536]{1,0:T(8,128)(2,1)}), bf16[512,1536]{1,0:T(8,128)(2,1)}) %all-gather.5.cloned.1.call-update) | async-done | bytes 1572880 | tf_op jit(solution)/shard_map/all_gather | solution.py:199
  50.0 2.6 fusion.31
  52.6 23.6 %all-gather.7.cloned.1.call-done = bf16[768,896]{1,0:T(8,128)(2,1)} async-done(((bf16[96,896]{1,0:T(8,128)(2,1)}), bf16[768,896]{1,0:T(8,128)(2,1)}) %all-gather.7.cloned.1.call-update) | async-done | bytes 1376272 | tf_op jit(solution)/shard_map/all_gather | solution.py:198
  80.2 6.6 %attention_forward.1 = (bf16[512,768]{1,0:T(8,128)(2,1)}, bf16[512,576]{1,0:T(8,128)(2,1)}, f32[3,512,512]{2,1,0:T(8,128)}, bf16[512,192]{1,0:T(8,128)(2,1)}, bf16[512,768]{1,0:T(8,128)(2,1)}) custom-call(bf16[512,768]{1,0:T(8,128)(2,1)} %get-tuple-element.110.refs_0_, f32[1,768]{1,0:T(1,128)} %reshape_squeeze.7.refs_1_.refs_8_, ...), custom_call_target="tpu_custom_call" | custom-call | flops 3000000000 | bytes 12000000 | tf_op jit(solution)/shard_map/attention_forward/pallas_call | solution.py:214
  88.7 21.6 %reduce-scatter.5.cloned.1.call-done = bf16[128,768]{1,0:T(8,128)(2,1)} async-done(((bf16[512,768]{1,0:T(8,128)(2,1)}), bf16[128,768]{1,0:T(8,128)(2,1)}) %reduce-scatter.5.cloned.1.call-update) | async-done | bytes 196624 | tf_op jit(solution)/shard_map/reduce_scatter | solution.py:226
  111.4 1.5 fusion.33
  114.7 19.6 %all_gather.20 = bf16[512,896]{1,0:T(8,128)(2,1)S(1)} all-gather(bf16[128,896]{1,0:T(8,128)(2,1)S(1)} %fusion.13), channel_id=1, replica_groups=mesh['dp'=8,'tensor'=4] {'tensor'}, dimensions={0}, use_global_device_ids=true | all-gather | bytes 1146880 | tf_op jit(solution)/shard_map/all_gather | solution.py:243
  136.2 14.0 %all-gather.9.cloned.1.call-done.refs_4_ = bf16[4,768,768]{2,1,0:T(8,128)(2,1)} async-done(((bf16[4,96,768]{2,1,0:T(8,128)(2,1)}), bf16[4,768,768]{2,1,0:T(8,128)(2,1)}) %all-gather.9.cloned.1.call-update) | async-done | bytes 4718608 | tf_op jit(solution)/shard_map/all_gather | solution.py:193
  150.2 40.7 %all-gather.11.cloned.1.call-done.refs_5_ = bf16[4,768,768]{2,1,0:T(8,128)(2,1)} async-done(((bf16[4,96,768]{2,1,0:T(8,128)(2,1)}), bf16[4,768,768]{2,1,0:T(8,128)(2,1)}) %all-gather.11.cloned.1.call-update) | async-done | bytes 4718608 | tf_op jit(solution)/shard_map/all_gather | solution.py:194
  190.9 15.0 %experts.1 = (bf16[512,768]{1,0:T(8,128)(2,1)}, bf16[512,768]{1,0:T(8,128)(2,1)}, bf16[4,768,768]{2,1,0:T(8,128)(2,1)}, bf16[4,768,768]{2,1,0:T(8,128)(2,1)}) custom-call(s32[1,512]{1,0:T(1,128)} %bitcast.31, bf16[512,768]{1,0:T(8,128)(2,1)} %slice.111.refs_1_, f32[512,1]{1,0:T(8,128)} %copy.65.refs_2_, bf16[512,768]{1,0:T(8,128)(2,1)} %get-tuple-element.109.refs_3_, ...), custom_call_target="tpu_custom_call" | custom-call | flops 6000000000 | bytes 12000000 | tf_op jit(solution)/shard_map/experts/pallas_call | solution.py:250
  205.9 8.1 %copy.69 = bf16[4,768,768]{2,0,1:T(4,128)(2,1)} copy(bf16[4,768,768]{2,1,0:T(8,128)(2,1)} %get-tuple-element.38) | data formatting | bytes 9437184 | tf_op jit(solution)/shard_map/experts/pallas_call | solution.py:250
  214.0 4.7 %all-to-all-start = ((bf16[4,768,768]{2,0,1:T(4,128)(2,1)}), bf16[4,768,768]{2,0,1:T(4,128)(2,1)}, u32[]{:S(2)}, u32[]{:S(2)}) async-start(bf16[4,768,768]{2,0,1:T(4,128)(2,1)} %copy.69), calls=%async_computation.4 | async-start | bytes 9437184 | tf_op jit(solution)/shard_map/all_to_all | solution.py:273
  218.8 1.3 pad_maximum_fusion
  220.2 8.2 %copy.70 = bf16[4,768,768]{2,0,1:T(4,128)(2,1)} copy(bf16[4,768,768]{2,1,0:T(8,128)(2,1)} %get-tuple-element.39) | data formatting | bytes 9437184 | tf_op jit(solution)/shard_map/experts/pallas_call | solution.py:250
  228.4 29.9 %reduce-scatter.7.cloned.1.call-done = bf16[128,1536]{1,0:T(8,128)(2,1)} async-done(((bf16[512,1536]{1,0:T(8,128)(2,1)}), bf16[128,1536]{1,0:T(8,128)(2,1)}) %reduce-scatter.7.cloned.1.call-update) | async-done | bytes 393232 | tf_op jit(solution)/shard_map/reduce_scatter | solution.py:276
  259.4 14.1 %all-to-all-done = bf16[4,768,768]{2,0,1:T(4,128)(2,1)} async-done(((bf16[4,768,768]{2,0,1:T(4,128)(2,1)}), bf16[4,768,768]{2,0,1:T(4,128)(2,1)}, u32[]{:S(2)}, u32[]{:S(2)}) %all-to-all-start) | async-done | bytes 4718624 | tf_op jit(solution)/shard_map/all_to_all | solution.py:273
  273.5 4.6 %all-to-all-start.1 = ((bf16[4,768,768]{2,0,1:T(4,128)(2,1)}), bf16[4,768,768]{2,0,1:T(4,128)(2,1)}, u32[]{:S(2)}, u32[]{:S(2)}) async-start(bf16[4,768,768]{2,0,1:T(4,128)(2,1)} %copy.70), calls=%async_computation.5 | async-start | bytes 9437184 | tf_op jit(solution)/shard_map/all_to_all | solution.py:274
  280.1 20.0 %all_gather.23.refs_5_ = bf16[512,768]{1,0:T(8,128)(2,1)} all-gather(bf16[128,768]{1,0:T(8,128)(2,1)S(1)} %fusion.27), channel_id=1, replica_groups=mesh['dp'=8,'tensor'=4] {'tensor'}, dimensions={0}, use_global_device_ids=true | all-gather | bytes 983040 | tf_op jit(solution)/shard_map/all_gather | solution.py:293
  300.1 9.6 %attention_backward.1 = (bf16[3,768,192]{2,1,0:T(8,128)(2,1)}, bf16[768,192]{1,0:T(8,128)(2,1)}, bf16[512,768]{1,0:T(8,128)(2,1)}, f32[1,768]{1,0:T(1,128)}, f32[8,32]{1,0:T(8,128)}) custom-call(bf16[512,768]{1,0:T(8,128)(2,1)} %get-tuple-element.110.refs_0_, bf16[512,768]{1,0:T(8,128)(2,1)} %get-tuple-element.29.refs_1_, ...), custom_call_target="tpu_custom_call" | custom-call | flops 4000000000 | bytes 12000000 | tf_op jit(solution)/shard_map/attention_backward/pallas_call | solution.py:295
  312.9 2.1 concatenate.32
  315.0 4.7 %convert_reduce_fusion.1 = f32[4,96,768]{2,0,1:T(4,128)S(1)} fusion(bf16[4,8,96,768]{3,0,2,1:T(4,128)(2,1)} %bitcast.13), kind=kLoop, calls=%fused_computation.1 | loop fusion | flops 4423680 | bytes 5898240 | tf_op jit(solution)/shard_map/reduce_sum | solution.py:331
  319.8 1.2 copy.72
  321.0 11.9 %all-to-all-done.1 = bf16[4,768,768]{2,0,1:T(4,128)(2,1)} async-done(((bf16[4,768,768]{2,0,1:T(4,128)(2,1)}), bf16[4,768,768]{2,0,1:T(4,128)(2,1)}, u32[]{:S(2)}, u32[]{:S(2)}) %all-to-all-start.1) | async-done | bytes 4718624 | tf_op jit(solution)/shard_map/all_to_all | solution.py:274
  332.9 4.7 %convert_reduce_fusion = f32[4,96,768]{2,0,1:T(4,128)S(1)} fusion(bf16[4,8,96,768]{3,0,2,1:T(4,128)(2,1)} %bitcast.14), kind=kLoop, calls=%fused_computation | loop fusion | flops 4423680 | bytes 5898240 | tf_op jit(solution)/shard_map/reduce_sum | solution.py:334
  337.5 1.2 copy.73
  338.8 1.1 fusion.3
  339.9 2.0 fusion.6
  341.9 31.4 %reduce-scatter.11.cloned.1.call-done = bf16[96,896]{1,0:T(8,128)(2,1)} async-done(((bf16[768,896]{1,0:T(8,128)(2,1)}), bf16[96,896]{1,0:T(8,128)(2,1)}) %reduce-scatter.11.cloned.1.call-update) | async-done | bytes 172048 | tf_op jit(solution)/shard_map/reduce_scatter | solution.py:318
  374.0 19.5 %psum.7 = f32[96,6]{1,0:T(8,128)S(1)} all-reduce(f32[96,6]{1,0:T(8,128)S(1)} %slice.116), channel_id=1, replica_groups=mesh['dp'=8,'tensor'=4] {'tensor'}, use_global_device_ids=true, to_apply=%region_14.15 | all-reduce | flops 576 | bytes 4608 | tf_op jit(solution)/shard_map/psum | solution.py:328
  396.6 1.7 fusion.32
  (94 shorter events, 23.1 us)
Async XLA Ops:
  7.2 4.5 %copy-start.11 = (bf16[3,32]{1,0:T(4,128)(2,1)S(1)}, bf16[3,32]{1,0:T(4,128)(2,1)}, u32[]{:S(2)}) copy-start(bf16[3,32]{1,0:T(4,128)(2,1)} %param.24) | copy-start | bytes 580
  7.2 5.1 %copy-start.8 = (s32[1023]{0:T(1024)S(1)}, s32[1023]{0:T(1024)}, u32[]{:S(2)}) copy-start(s32[1023]{0:T(1024)} %param.17) | copy-start | bytes 12280
  7.2 42.8 %all-gather.5.cloned.1.call-start = ((), (), s32[]{:S(2)}) async-start(), calls=%async_computation.6 | async-start | bytes 1966080 | tf_op jit(solution)/shard_map/all_gather | solution.py:199
  9.1 67.2 %all-gather.7.cloned.1.call-start = ((), (), s32[]{:S(2)}) async-start(), calls=%async_computation.7 | async-start | bytes 1548288 | tf_op jit(solution)/shard_map/all_gather | solution.py:198
  11.7 98.6 %reduce-scatter.5.cloned.1.call-start = ((), (), s32[]{:S(2)}) async-start(), calls=%async_computation.8 | async-start | bytes 983040 | tf_op jit(solution)/shard_map/reduce_scatter | solution.py:226
  76.2 2.1 copy-start.3
  86.8 23.5 %copy-start = (bf16[128,768]{1,0:T(8,128)(2,1)S(1)}, bf16[128,768]{1,0:T(8,128)(2,1)}, u32[]{:S(2)}) copy-start(bf16[128,768]{1,0:T(8,128)(2,1)} %param.14) | copy-start | bytes 589828
  86.8 63.4 %all-gather.9.cloned.1.call-start = ((), (), s32[]{:S(2)}) async-start(), calls=%async_computation.9 | async-start | bytes 5308416 | tf_op jit(solution)/shard_map/all_gather | solution.py:193
  87.4 103.5 %all-gather.11.cloned.1.call-start = ((), (), s32[]{:S(2)}) async-start(), calls=%async_computation.10 | async-start | bytes 5308416 | tf_op jit(solution)/shard_map/all_gather | solution.py:194
  88.7 24.8 %copy-start.12 = (s32[128]{0:T(128)}, s32[128]{0:T(128)S(1)}, u32[]{:S(2)}) copy-start(s32[128]{0:T(128)S(1)} %dynamic-slice_bitcast_fusion) | copy-start | bytes 1540
  214.0 4.8 %copy-start.5 = (bf16[512,768]{1,0:T(8,128)(2,1)S(1)}, bf16[512,768]{1,0:T(8,128)(2,1)}, u32[]{:S(2)}) copy-start(bf16[512,768]{1,0:T(8,128)(2,1)} %get-tuple-element.27) | copy-start | bytes 2359300
  214.0 4.8 %copy-start.6 = (bf16[512,768]{1,0:T(8,128)(2,1)S(1)}, bf16[512,768]{1,0:T(8,128)(2,1)}, u32[]{:S(2)}) copy-start(bf16[512,768]{1,0:T(8,128)(2,1)} %get-tuple-element.28) | copy-start | bytes 2359300
  214.0 59.5 %all-to-all-start = ((bf16[4,768,768]{2,0,1:T(4,128)(2,1)}), bf16[4,768,768]{2,0,1:T(4,128)(2,1)}, u32[]{:S(2)}, u32[]{:S(2)}) async-start(bf16[4,768,768]{2,0,1:T(4,128)(2,1)} %copy.69), calls=%async_computation.4 | async-start | bytes 9437184 | tf_op jit(solution)/shard_map/all_to_all | solution.py:273
  218.8 39.5 %reduce-scatter.7.cloned.1.call-start = ((), (), s32[]{:S(2)}) async-start(), calls=%async_computation.11 | async-start | bytes 1966080 | tf_op jit(solution)/shard_map/reduce_scatter | solution.py:276
  259.3 19.1 %copy-start.1 = (bf16[128,768]{1,0:T(8,128)(2,1)S(1)}, bf16[128,768]{1,0:T(8,128)(2,1)}, u32[]{:S(2)}) copy-start(bf16[128,768]{1,0:T(8,128)(2,1)} %reduce-scatter.5.cloned.1.call-done) | copy-start | bytes 589828
  259.3 19.1 %copy-start.2 = (bf16[128,768]{1,0:T(8,128)(2,1)S(1)}, bf16[128,768]{1,0:T(8,128)(2,1)}, u32[]{:S(2)}) copy-start(bf16[128,768]{1,0:T(8,128)(2,1)} %param.15) | copy-start | bytes 589828
  259.4 19.9 %copy-start.10 = (f32[128,4]{0,1:T(4,128)S(1)}, f32[128,4]{0,1:T(4,128)}, u32[]{:S(2)}) copy-start(f32[128,4]{0,1:T(4,128)} %get-tuple-element.108) | copy-start | bytes 6148
  259.4 19.9 %copy-start.13 = (s32[128]{0:T(128)S(1)}, s32[128]{0:T(128)}, u32[]{:S(2)}) copy-start(s32[128]{0:T(128)} %copy-done.12) | copy-start | bytes 1540
  273.5 59.4 %all-to-all-start.1 = ((bf16[4,768,768]{2,0,1:T(4,128)(2,1)}), bf16[4,768,768]{2,0,1:T(4,128)(2,1)}, u32[]{:S(2)}, u32[]{:S(2)}) async-start(bf16[4,768,768]{2,0,1:T(4,128)(2,1)} %copy.70), calls=%async_computation.5 | async-start | bytes 9437184 | tf_op jit(solution)/shard_map/all_to_all | solution.py:274
  278.1 60.6 %reduce-scatter.9.cloned.1.call-start = ((), (), s32[]{:S(2)}) async-start(), calls=%async_computation.12 | async-start | bytes 983040 | tf_op jit(solution)/shard_map/reduce_scatter | solution.py:307
  309.7 1.6 copy-start.9
  309.7 63.5 %reduce-scatter.11.cloned.1.call-start = ((), (), s32[]{:S(2)}) async-start(), calls=%async_computation.13 | async-start | bytes 1548288 | tf_op jit(solution)/shard_map/reduce_scatter | solution.py:318
  311.5 1.3 copy-start.4
  311.8 1.1 copy-start.7
Sparse Core Ops, SparseCore 0:
  10.2 39.7 all-gather.4
  52.5 23.7 all-gather.6
  86.9 23.2 reduce-scatter.4
  112.0 38.1 all-gather.8
  152.0 38.9 all-gather.10
  221.6 36.6 reduce-scatter.6
  309.8 23.1 reduce-scatter.8
  336.3 36.8 reduce-scatter.10

commit v2 on v1

--- a/solution.py
+++ b/solution.py
@@ -127,7 +127,39 @@
     gain_grad[...] = jnp.sum(grad_na * (x * r1), axis=0, keepdims=True)
 
 
-def ffn_kernel(cap, routes, rows, gating, cot, up, down, ret, gnf, gup, gdown, gret):
+def turn(x, k):
+    n = lax.axis_size("tensor")
+    return lax.ppermute(x, "tensor", [(i, (i + k) % n) for i in range(n)])
+
+
+def gather_rows(x):
+    n, me, rows = lax.axis_size("tensor"), lax.axis_index("tensor"), x.shape[0]
+    out = jnp.zeros((n * rows, x.shape[1]), x.dtype)
+    for k in range(n):
+        block = x if k == 0 else turn(x, k)
+        out = lax.dynamic_update_slice_in_dim(out, block, lax.rem(me + n - k, n) * rows, 0)
+    return out
+
+
+def scatter_rows(x):
+    n, me = lax.axis_size("tensor"), lax.axis_index("tensor")
+    rows = x.shape[0] // n
+    total = lax.dynamic_slice_in_dim(x, me * rows, rows, 0).astype(F32)
+    for k in range(1, n):
+        piece = lax.dynamic_slice_in_dim(x, lax.rem(me + k, n) * rows, rows, 0)
+        total = total + turn(piece, k).astype(F32)
+    return total
+
+
+def store_grad(grads, which, value, shard):
+    if shard is None:
+        grads[which, 0] = value
+        return
+    for o in range(grads.shape[0]):
+        grads[o, which, 0] = value[o * shard : (o + 1) * shard]
+
+
+def ffn_kernel(cap, shard, routes, rows, gating, cot, up, down, ret, gnf, grads, gret):
     e = pl.program_id(0)
     length, model = rows.shape
 
@@ -156,8 +188,8 @@
         1.0 + 3.0 * GELU_B * pre * pre
     )
     gpre = (slope * dot(gslot, downw)).astype(BF)
-    gdown[0] = dot(gslot, act, 0, 0).astype(BF)
-    gup[0] = dot(disp, gpre, 0, 0).astype(BF)
+    store_grad(grads, 1, dot(gslot, act, 0, 0).astype(BF), shard)
+    store_grad(grads, 0, dot(disp, gpre, 0, 0).astype(BF), shard)
     out = dot(act, downw, 1, 1).astype(BF)
     ret[...] += dot(place, out, 0, 0).astype(BF)
     back = dot(gpre, upw, 1, 1).astype(BF)
@@ -196,10 +228,9 @@
     small = jnp.pad(small, ((0, 0), (0, SMALL - small.shape[1])))
     pack = jnp.concatenate([w_query, w_key, w_value, w_output, small], axis=1)
     pack = lax.all_gather(pack, "dp", axis=0, tiled=True)
-    both = lax.all_gather(
-        jnp.concatenate([tokens, cotangent], axis=1), "tensor", axis=0, tiled=True
-    )
-    tok_all, cot_all = both[:, :model], both[:, model:]
+    pack, up_full = lax.optimization_barrier((pack, up_full))
+    tok_all = gather_rows(tokens)
+    cot_all = gather_rows(cotangent)
     wqkv, wout = pack[:, : 3 * width], pack[:, 3 * width : 4 * width]
     small = pack[:, 4 * width :].astype(F32)
     gain_one = small[:, 0].reshape(1, model)
@@ -223,10 +254,10 @@
         3_000_000_000,
         name="attention_forward",
     )(tok_all, gain_one, wqkv, wout, table8, bucket_row)
-    attended = lax.psum_scatter(part, "tensor", scatter_dimension=0, tiled=True)
+    attended = scatter_rows(part)
 
     token_rows = tokens.astype(F32)
-    hidden = token_rows + attended.astype(F32)
+    hidden = token_rows + attended
     route_all = routes[:, 0]
     route_mine = lax.dynamic_slice_in_dim(
         route_all, lax.axis_index("tensor") * local_rows, local_rows
@@ -247,13 +278,20 @@
 
     whole = lambda *shape: pl.BlockSpec(shape, lambda e: (0,) * len(shape))
     per_expert = pl.BlockSpec((1, model, hidden_here), lambda e: (e, 0, 0))
-    ret, gnf, grad_up, grad_down = call(
-        lambda *refs: ffn_kernel(CAP, *refs),
+    owners = lax.axis_size("dp")
+    if shard % 16 == 0:
+        grads_shape = (owners, 2, experts, shard, hidden_here)
+        grads_spec = pl.BlockSpec((owners, 2, 1, shard, hidden_here), lambda e: (0, 0, e, 0, 0))
+    else:
+        grads_shape = (2, experts, model, hidden_here)
+        grads_spec = pl.BlockSpec((2, 1, model, hidden_here), lambda e: (0, e, 0, 0))
+    cut = shard if shard % 16 == 0 else None
+    ret, gnf, grads = call(
+        lambda *refs: ffn_kernel(CAP, cut, *refs),
         (
             sds((length, model)),
             sds((length, model)),
-            sds((experts, model, hidden_here)),
-            sds((experts, model, hidden_here)),
+            sds(grads_shape),
         ),
         6_000_000_000,
         name="experts",
@@ -266,12 +304,22 @@
             per_expert,
             per_expert,
         ],
-        out_specs=[whole(length, model), whole(length, model), per_expert, per_expert],
+        out_specs=[whole(length, model), whole(length, model), grads_spec],
         scratch_shapes=[pltpu.VMEM((length, model), BF)],
     )(route_all[None, :], nf_all[:, :model], gate_all, cot_all, up_full, down_full)
 
-    traded_up = lax.all_to_all(grad_up, "dp", split_axis=1, concat_axis=0, tiled=True)
-    traded_down = lax.all_to_all(grad_down, "dp", split_axis=1, concat_axis=0, tiled=True)
+    if cut is None:
+        grads = grads.reshape(2, experts, owners, shard, hidden_here).transpose(2, 0, 1, 3, 4)
+    if owners <= 16:
+        place = lax.axis_index("dp")
+        traded = [lax.dynamic_index_in_dim(grads, place, 0, keepdims=False)]
+        for k in range(1, owners):
+            piece = lax.dynamic_index_in_dim(grads, lax.rem(place + k, owners), 0, keepdims=False)
+            pairs = [(i, (i + k) % owners) for i in range(owners)]
+            traded.append(lax.ppermute(piece, "dp", pairs))
+    else:
+        traded = lax.all_to_all(grads, "dp", split_axis=0, concat_axis=0, tiled=True)
+        traded = [traded[i] for i in range(owners)]
 
     summed = lax.psum_scatter(
         jnp.concatenate([ret, gnf], axis=1), "tensor", scatter_dimension=0, tiled=True
@@ -304,7 +352,7 @@
         4_000_000_000,
         name="attention_backward",
     )(tok_all, na, qkv, probs, ctx, gh_all, wqkv, wout, gain_one, bucket_row)
-    grad_na = lax.psum_scatter(gna, "tensor", scatter_dimension=0, tiled=True).astype(F32)
+    grad_na = scatter_rows(gna)
     r1 = lax.rsqrt(jnp.mean(token_rows * token_rows, axis=-1, keepdims=True) + EPS)
     u1 = token_rows * r1
     gn1 = grad_na * gain_one
@@ -321,25 +369,23 @@
         scatter_dimension=0,
         tiled=True,
     ).astype(F32)
-    grads = [summed[:, i * width : (i + 1) * width] for i in range(4)]
+    squares = [summed[:, i * width : (i + 1) * width] for i in range(4)]
     smalls = summed[:, 4 * width :]
     start = 2 + experts
     grad_table = smalls[0, start : start + heads * count].reshape(heads, count)
-    total = lax.psum(smalls[:, :start], "tensor")
-
-    owners = lax.axis_size("dp")
-    sum_up = jnp.sum(
-        traded_up.reshape(owners, experts, shard, hidden_here).astype(F32), axis=0
-    )
-    sum_down = jnp.sum(
-        traded_down.reshape(owners, experts, shard, hidden_here).astype(F32), axis=0
-    )
+    mine = smalls[:, :start]
+    total = mine
+    for k in range(1, lax.axis_size("tensor")):
+        total = total + turn(mine, k)
+
+    sum_up = sum(part[0].astype(F32) for part in traded)
+    sum_down = sum(part[1].astype(F32) for part in traded)
     return (
         layer_out,
         grad_tokens,
         total[:, 0],
         total[:, 1],
-        *grads,
+        *squares,
         grad_table,
         total[:, 2:start],
         sum_up,

time: 406 us -> 298 us (0.73)
  waiting for transfers between devices: 225 us -> 129 us
  starting transfers between devices: 9.89 us -> 30.3 us
  blocking collectives: 59.1 us -> 41.8 us
  local copies, waits for them, and re-layouts: 39.2 us -> 31.8 us
  other arithmetic: 23.5 us -> 16.7 us
    ppermute x0 -> x22, waiting for transfers between devices: none -> 62.5 us  [the longest x7 39 us: per_device(): traded.append(lax.ppermute(piece, 'dp', pairs))]
    all_gather x1, waiting for transfers between devices: 40.7 us -> 0.01 us  [per_device(): down_full = lax.all_gather(expert_down, 'dp', axis=1, tiled=True)]
    all_gather x1 -> x0, waiting for transfers between devices: 37.1 us -> none  [per_device(): lax.all_gather(jnp.concatenate([tokens, cotangent], axis=1), 'tensor', ax...]
    reduce_scatter x1, waiting for transfers between devices: 31.4 us -> 0.41 us  [per_device(): lax.psum_scatter(jnp.concatenate([gw[0], gw[1], gw[2], gout, cols], axis=...]
    ppermute x0 -> x22, starting transfers between devices: none -> 30.1 us  [the longest x15 23.3 us: turn(): return lax.ppermute(x, 'tensor', [(i, (i + k) % n) for i in range(n)])]
    all_gather x1, waiting for transfers between devices: 14 us -> 40.9 us  [per_device(): up_full = lax.all_gather(expert_up, 'dp', axis=1, tiled=True)]
    all_to_all x2 -> x0, waiting for transfers between devices: 26 us -> none  [the longest x1 14.1 us: per_device(): lax.all_to_all(grad_up, 'dp', split_axis=1, concat_axis=0, tiled=True)]
    all_gather x1, waiting for transfers between devices: 23.6 us -> 1.57 us  [per_device(): pack = lax.all_gather(pack, 'dp', axis=0, tiled=True)]
  transfers between devices with their start and end apart: 10 -> 27, of which waited for: 9 -> 10; matrix products, arithmetic and copies ran while one was open for 11% -> 14% of each run, Pallas kernels for 2% -> 5%
where the time goes in v2:
time: 298 us
  waiting for transfers between devices  129 us (43%)
  blocking collectives  41.8 us (14%)
  Pallas kernels  31.9 us (11%)
  local copies, waits for them, and re-layouts  31.8 us (11%)
  starting transfers between devices  30.3 us (10%)
  other arithmetic  16.7 us (6%)
  between operations  14.2 us (5%)
    all_gather x1, waiting for transfers between devices, per_device(): up_full = lax.all_gather(expert_up, 'dp', axis=1, tiled=True)  40.9 us
    ppermute x7, waiting for transfers between devices, per_device(): traded.append(lax.ppermute(piece, 'dp', pairs))  39 us
    ppermute x15, waiting for transfers between devices, turn(): return lax.ppermute(x, 'tensor', [(i, (i + k) % n) for i in range(n)])  23.5 us
    all_gather x1, blocking collectives, per_device(): lax.all_gather(jnp.concatenate([nf.astype(BF), gate_cols], axis=1), 'tens...  23.3 us
    ppermute x15, starting transfers between devices, turn(): return lax.ppermute(x, 'tensor', [(i, (i + k) % n) for i in range(n)])  23.3 us
    reduce_scatter x1, waiting for transfers between devices, per_device(): lax.psum_scatter(jnp.concatenate([ret, gnf], axis=1), 'tensor', scatter_d...  22.4 us
    all_gather x1, blocking collectives, per_device(): lax.all_gather(grad_hidden.astype(BF), 'tensor', axis=0, tiled=True)  18.5 us
    pallas_call x1, Pallas kernels, per_device(): call(lambda *refs: ffn_kernel(CAP, cut, *refs), (sds((length, model)), sd...  15.7 us
  transfers between devices with their start and end apart: 27, of which 10 were waited for; matrix products, arithmetic and copies ran while one was open for 14% of the time, Pallas kernels for 5%

profile of v2, /device:TPU:0, one launch (start us, length us, event | category | flops | bytes accessed | tf_op | source)
XLA Modules:
  0.0 297.5 jit_solution(17364708453554137338)
XLA Ops:
  8.2 1.7 concatenate.23
  11.5 3.1 %collective-permute-start = (bf16[128,768]{1,0:T(8,128)(2,1)S(1)}, bf16[128,768]{1,0:T(8,128)(2,1)S(1)}, u32[]{:S(2)}, u32[]{:S(2)}) collective-permute-start(bf16[128,768]{1,0:T(8,128)(2,1)S(1)} %copy-done.1), channel_id=1, source_target_pairs={{0,1},{1,2},{2,3},{3,0},{4,5},{5,6},{6,7},{7,4},{8,9},{9,10},{10,1... | collective-permute-start | bytes 589832 | tf_op jit(solution)/shard_map/ppermute | solution.py:132
  14.6 2.6 collective-permute-start.1
  23.1 2.8 collective-permute-start.8
  26.6 8.5 %collective-permute-done.6 = bf16[128,768]{1,0:T(8,128)(2,1)S(1)} collective-permute-done((bf16[128,768]{1,0:T(8,128)(2,1)S(1)}, bf16[128,768]{1,0:T(8,128)(2,1)S(1)}, u32[]{:S(2)}, u32[]{:S(2)}) %collective-permute-start.6) | collective-permute-done | bytes 196640 | tf_op jit(solution)/shard_map/ppermute | solution.py:132
  36.5 1.6 all-gather.4.cloned.1.call-done
  38.1 40.9 %all-gather.6.cloned.1.call-done.refs_4_ = bf16[4,768,768]{2,1,0:T(8,128)(2,1)} async-done(((bf16[4,96,768]{2,1,0:T(8,128)(2,1)}), bf16[4,768,768]{2,1,0:T(8,128)(2,1)}) %all-gather.6.cloned.1.call-update) | async-done | bytes 4718608 | tf_op jit(solution)/shard_map/all_gather | solution.py:225
  79.0 2.2 slice.125.refs_2_.refs_6_
  83.1 6.6 %attention_forward.1 = (bf16[512,768]{1,0:T(8,128)(2,1)}, bf16[512,576]{1,0:T(8,128)(2,1)}, f32[3,512,512]{2,1,0:T(8,128)}, bf16[512,192]{1,0:T(8,128)(2,1)}, bf16[512,768]{1,0:T(8,128)(2,1)}) custom-call(bf16[512,768]{1,0:T(8,128)(2,1)} %constant_dynamic-update-slice_fusion.4.refs_0_, f32[1,768]{1,0:T(1,128)} %reshape_squeeze.7.refs_1_.refs_8_, ...), custom_call_target="tpu_custom_call" | custom-call | flops 3000000000 | bytes 12000000 | tf_op jit(solution)/shard_map/attention_forward/pallas_call | solution.py:245
  90.9 1.5 collective-permute-start.3
  92.4 2.4 collective-permute-start.4
  94.8 1.4 collective-permute-start.5
  96.3 4.3 %collective-permute-done.3 = bf16[128,768]{1,0:T(8,128)(2,1)S(1)} collective-permute-done((bf16[128,768]{1,0:T(8,128)(2,1)S(1)}, bf16[128,768]{1,0:T(8,128)(2,1)S(1)}, u32[]{:S(2)}, u32[]{:S(2)}) %collective-permute-start.3) | collective-permute-done | bytes 196640 | tf_op jit(solution)/shard_map/ppermute | solution.py:132
  100.6 7.8 %collective-permute-done.4 = bf16[128,768]{1,0:T(8,128)(2,1)S(1)} collective-permute-done((bf16[128,768]{1,0:T(8,128)(2,1)S(1)}, bf16[128,768]{1,0:T(8,128)(2,1)S(1)}, u32[]{:S(2)}, u32[]{:S(2)}) %collective-permute-start.4) | collective-permute-done | bytes 196640 | tf_op jit(solution)/shard_map/ppermute | solution.py:132
  110.5 23.3 %all_gather.17 = bf16[512,896]{1,0:T(8,128)(2,1)S(1)} all-gather(bf16[128,896]{1,0:T(8,128)(2,1)S(1)} %fusion.14), channel_id=1, replica_groups=mesh['dp'=8,'tensor'=4] {'tensor'}, dimensions={0}, use_global_device_ids=true | all-gather | bytes 1146880 | tf_op jit(solution)/shard_map/all_gather | solution.py:274
  135.7 15.7 %experts.1 = (bf16[512,768]{1,0:T(8,128)(2,1)}, bf16[512,768]{1,0:T(8,128)(2,1)}, bf16[8,2,4,96,768]{4,3,2,1,0:T(8,128)(2,1)}) custom-call(s32[1,512]{1,0:T(1,128)} %bitcast.121, bf16[512,768]{1,0:T(8,128)(2,1)} %slice.164.refs_1_, f32[512,1]{1,0:T(8,128)} %copy.52.refs_2_, bf16[512,768]{1,0:T(8,128)(2,1)} %copy-done.5, ...), custom_call_target="tpu_custom_call" | custom-call | flops 6000000000 | bytes 12000000 | tf_op jit(solution)/shard_map/experts/pallas_call | solution.py:289
  151.4 2.7 pad_maximum_fusion
  154.3 6.7 %dynamic-slice_bitcast_fusion.6 = (bf16[2,4,96,768]{3,2,1,0:T(8,128)(2,1)}, bf16[2,4,96,768]{3,2,1,0:T(8,128)(2,1)}, bf16[2,4,96,768]{3,2,1,0:T(8,128)(2,1)}, bf...) fusion(bf16[8,2,4,96,768]{4,3,2,1,0:T(8,128)(2,1)} %get-tuple-e, ...), kind=kLoop, calls=%fused_computation.22 | loop fusion | bytes 16515100 | tf_op jit(solution)/shard_map/jit(dynamic_index_in_dim)/squeeze | solution.py:317
  161.0 1.5 collective-permute-start.16
  162.5 1.5 collective-permute-start.17
  165.4 22.4 %reduce-scatter.3.cloned.1.call-done = bf16[128,1536]{1,0:T(8,128)(2,1)} async-done(((bf16[512,1536]{1,0:T(8,128)(2,1)}), bf16[128,1536]{1,0:T(8,128)(2,1)}) %reduce-scatter.3.cloned.1.call-update) | async-done | bytes 393232 | tf_op jit(solution)/shard_map/reduce_scatter | solution.py:324
  191.1 18.5 %all_gather.19.refs_5_ = bf16[512,768]{1,0:T(8,128)(2,1)} all-gather(bf16[128,768]{1,0:T(8,128)(2,1)S(1)} %fusion.31), channel_id=1, replica_groups=mesh['dp'=8,'tensor'=4] {'tensor'}, dimensions={0}, use_global_device_ids=true | all-gather | bytes 983040 | tf_op jit(solution)/shard_map/all_gather | solution.py:341
  209.6 9.6 %attention_backward.1 = (bf16[3,768,192]{2,1,0:T(8,128)(2,1)}, bf16[768,192]{1,0:T(8,128)(2,1)}, bf16[512,768]{1,0:T(8,128)(2,1)}, f32[1,768]{1,0:T(1,128)}, f32[8,32]{1,0:T(8,128)}) custom-call(bf16[512,768]{1,0:T(8,128)(2,1)} %constant_dynamic-update-slice_fusion.4.refs_0_, bf16[512,768]{1,0:T(8,128)(2,1)} %get-tuple-element.32.refs_1_, ...), custom_call_target="tpu_custom_call" | custom-call | flops 4000000000 | bytes 12000000 | tf_op jit(solution)/shard_map/attention_backward/pallas_call | solution.py:343
  221.4 2.4 collective-permute-start.20
  224.9 2.1 concatenate.28
  228.1 12.8 %collective-permute-done.17 = bf16[2,4,96,768]{3,2,1,0:T(8,128)(2,1)} collective-permute-done((bf16[2,4,96,768]{3,2,1,0:T(8,128)(2,1)}, bf16[2,4,96,768]{3,2,1,0:T(8,128)(2,1)}, u32[]{:S(2)}, u32[]{:S(2)}) %collective-permute-start.17) | collective-permute-done | bytes 1179680 | tf_op jit(solution)/shard_map/ppermute | solution.py:319
  242.7 26.2 %collective-permute-done.19 = bf16[2,4,96,768]{3,2,1,0:T(8,128)(2,1)} collective-permute-done((bf16[2,4,96,768]{3,2,1,0:T(8,128)(2,1)}, bf16[2,4,96,768]{3,2,1,0:T(8,128)(2,1)}, u32[]{:S(2)}, u32[]{:S(2)}) %collective-permute-start.19) | collective-permute-done | bytes 1179680 | tf_op jit(solution)/shard_map/ppermute | solution.py:319
  268.9 6.5 %convert_add_fusion = (f32[4,96,768]{2,1,0:T(8,128)}, f32[4,96,768]{2,1,0:T(8,128)}) fusion(bf16[2,4,96,768]{3,2,1,0:T(8,128)(2,1)} %collective-permute-done.21, bf16[2,4,96,768]{3,2,1,0:T(8,128)(2,1)} %collective-permute-done.20, bf16[2,4,96,768]{3,2,1,0:T(8,128)(2,1)} %collective-permute-done.19, bf16[2,4,96,768]{3,2,1,0:T(8,128)(2,1)} %collective-permute-done.18, ...), kind=kLoop, calls=%fused_computation.2 | loop fusion | flops 8847360 | bytes 11796488 | tf_op jit(solution)/shard_map/add | solution.py:382
  275.4 2.9 collective-permute-done.9
  280.8 1.5 collective-permute-start.12
  282.3 2.4 collective-permute-start.13
  287.0 1.7 fusion.33
  (121 shorter events, 35.5 us)
Async XLA Ops:
  7.2 11.3 %copy-start = (bf16[128,768]{1,0:T(8,128)(2,1)S(1)}, bf16[128,768]{1,0:T(8,128)(2,1)}, u32[]{:S(2)}) copy-start(bf16[128,768]{1,0:T(8,128)(2,1)} %param.15) | copy-start | bytes 589828
  7.2 12.3 %copy-start.7 = (s32[1023]{0:T(1024)S(1)}, s32[1023]{0:T(1024)}, u32[]{:S(2)}) copy-start(s32[1023]{0:T(1024)} %param.17) | copy-start | bytes 12280
  7.2 12.9 %copy-start.8 = (bf16[3,32]{1,0:T(4,128)(2,1)S(1)}, bf16[3,32]{1,0:T(4,128)(2,1)}, u32[]{:S(2)}) copy-start(bf16[3,32]{1,0:T(4,128)(2,1)} %param.24) | copy-start | bytes 580
  7.2 30.9 %all-gather.4.cloned.1.call-start = ((), (), s32[]{:S(2)}) async-start(), calls=%async_computation.2 | async-start | bytes 1548288 | tf_op jit(solution)/shard_map/all_gather | solution.py:230
  9.9 69.0 %all-gather.6.cloned.1.call-start = ((), (), s32[]{:S(2)}) async-start(), calls=%async_computation.3 | async-start | bytes 5308416 | tf_op jit(solution)/shard_map/all_gather | solution.py:225
  10.7 125.1 %all-gather.8.cloned.1.call-start = ((), (), s32[]{:S(2)}) async-start(), calls=%async_computation.4 | async-start | bytes 5308416 | tf_op jit(solution)/shard_map/all_gather | solution.py:226
  11.4 176.4 %reduce-scatter.3.cloned.1.call-start = ((), (), s32[]{:S(2)}) async-start(), calls=%async_computation.5 | async-start | bytes 1966080 | tf_op jit(solution)/shard_map/reduce_scatter | solution.py:324
  11.5 11.6 %collective-permute-start = (bf16[128,768]{1,0:T(8,128)(2,1)S(1)}, bf16[128,768]{1,0:T(8,128)(2,1)S(1)}, u32[]{:S(2)}, u32[]{:S(2)}) collective-permute-start(bf16[128,768]{1,0:T(8,128)(2,1)S(1)} %copy-done.1), channel_id=1, source_target_pairs={{0,1},{1,2},{2,3},{3,0},{4,5},{5,6},{6,7},{7,4},{8,9},{9,10},{10,1... | collective-permute-start | bytes 589832 | tf_op jit(solution)/shard_map/ppermute | solution.py:132
  14.6 20.6 %collective-permute-start.1 = (bf16[128,768]{1,0:T(8,128)(2,1)S(1)}, bf16[128,768]{1,0:T(8,128)(2,1)S(1)}, u32[]{:S(2)}, u32[]{:S(2)}) collective-permute-start(bf16[128,768]{1,0:T(8,128)(2,1)S(1)} %copy-done.1), channel_id=1, source_target_pairs={{0,2},{1,3},{2,0},{3,1},{4,6},{5,7},{6,4},{7,5},{8,10},{9,11},{10,... | collective-permute-start | bytes 589832 | tf_op jit(solution)/shard_map/ppermute | solution.py:132
  17.1 18.7 %collective-permute-start.2 = (bf16[128,768]{1,0:T(8,128)(2,1)S(1)}, bf16[128,768]{1,0:T(8,128)(2,1)S(1)}, u32[]{:S(2)}, u32[]{:S(2)}) collective-permute-start(bf16[128,768]{1,0:T(8,128)(2,1)S(1)} %copy-done.1), channel_id=1, source_target_pairs={{0,3},{1,0},{2,1},{3,2},{4,7},{5,4},{6,5},{7,6},{8,11},{9,8},{10,9... | collective-permute-start | bytes 589832 | tf_op jit(solution)/shard_map/ppermute | solution.py:132
  18.5 16.6 %collective-permute-start.6 = (bf16[128,768]{1,0:T(8,128)(2,1)S(1)}, bf16[128,768]{1,0:T(8,128)(2,1)S(1)}, u32[]{:S(2)}, u32[]{:S(2)}) collective-permute-start(bf16[128,768]{1,0:T(8,128)(2,1)S(1)} %copy-done), channel_id=1, source_target_pairs={{0,1},{1,2},{2,3},{3,0},{4,5},{5,6},{6,7},{7,4},{8,9},{9,10},{10,1... | collective-permute-start | bytes 589832 | tf_op jit(solution)/shard_map/ppermute | solution.py:132
  19.2 77.1 %collective-permute-start.7 = (bf16[128,768]{1,0:T(8,128)(2,1)S(1)}, bf16[128,768]{1,0:T(8,128)(2,1)S(1)}, u32[]{:S(2)}, u32[]{:S(2)}) collective-permute-start(bf16[128,768]{1,0:T(8,128)(2,1)S(1)} %copy-done), channel_id=1, source_target_pairs={{0,2},{1,3},{2,0},{3,1},{4,6},{5,7},{6,4},{7,5},{8,10},{9,11},{10,... | collective-permute-start | bytes 589832 | tf_op jit(solution)/shard_map/ppermute | solution.py:132
  23.1 73.2 %collective-permute-start.8 = (bf16[128,768]{1,0:T(8,128)(2,1)S(1)}, bf16[128,768]{1,0:T(8,128)(2,1)S(1)}, u32[]{:S(2)}, u32[]{:S(2)}) collective-permute-start(bf16[128,768]{1,0:T(8,128)(2,1)S(1)} %copy-done), channel_id=1, source_target_pairs={{0,3},{1,0},{2,1},{3,2},{4,7},{5,4},{6,5},{7,6},{8,11},{9,8},{10,9... | collective-permute-start | bytes 589832 | tf_op jit(solution)/shard_map/ppermute | solution.py:132
  38.1 43.1 %copy-start.2 = (bf16[768,896]{1,0:T(8,128)(2,1)S(1)}, bf16[768,896]{1,0:T(8,128)(2,1)}, u32[]{:S(2)}) copy-start(bf16[768,896]{1,0:T(8,128)(2,1)} %all-gather.4.cloned.1.call-done) | copy-start | bytes 4128772
  90.9 9.7 %collective-permute-start.3 = (bf16[128,768]{1,0:T(8,128)(2,1)S(1)}, bf16[128,768]{1,0:T(8,128)(2,1)S(1)}, u32[]{:S(2)}, u32[]{:S(2)}) collective-permute-start(bf16[128,768]{1,0:T(8,128)(2,1)S(1)} %get-tuple-element.117), channel_id=1, source_target_pairs={{0,1},{1,2},{2,3},{3,0},{4,5},{5,6},{6,7},{7,4},{8,9},{9,10},{10,1... | collective-permute-start | bytes 589832 | tf_op jit(solution)/shard_map/ppermute | solution.py:132
  92.4 15.9 %collective-permute-start.4 = (bf16[128,768]{1,0:T(8,128)(2,1)S(1)}, bf16[128,768]{1,0:T(8,128)(2,1)S(1)}, u32[]{:S(2)}, u32[]{:S(2)}) collective-permute-start(bf16[128,768]{1,0:T(8,128)(2,1)S(1)} %get-tuple-element.119), channel_id=1, source_target_pairs={{0,2},{1,3},{2,0},{3,1},{4,6},{5,7},{6,4},{7,5},{8,10},{9,11},{10,... | collective-permute-start | bytes 589832 | tf_op jit(solution)/shard_map/ppermute | solution.py:132
  94.8 13.5 %collective-permute-start.5 = (bf16[128,768]{1,0:T(8,128)(2,1)S(1)}, bf16[128,768]{1,0:T(8,128)(2,1)S(1)}, u32[]{:S(2)}, u32[]{:S(2)}) collective-permute-start(bf16[128,768]{1,0:T(8,128)(2,1)S(1)} %get-tuple-element.118), channel_id=1, source_target_pairs={{0,3},{1,0},{2,1},{3,2},{4,7},{5,4},{6,5},{7,6},{8,11},{9,8},{10,9... | collective-permute-start | bytes 589832 | tf_op jit(solution)/shard_map/ppermute | solution.py:132
  96.3 14.1 %copy-start.5 = (bf16[512,768]{1,0:T(8,128)(2,1)}, bf16[512,768]{1,0:T(8,128)(2,1)S(1)}, u32[]{:S(2)}) copy-start(bf16[512,768]{1,0:T(8,128)(2,1)S(1)} %constant_dynamic-update-slice_fusion.refs_3_) | copy-start | bytes 2359300
  154.2 125.8 %reduce-scatter.5.cloned.1.call-start = ((), (), s32[]{:S(2)}) async-start(), calls=%async_computation.6 | async-start | bytes 1548288 | tf_op jit(solution)/shard_map/reduce_scatter | solution.py:366
  161.0 60.4 %collective-permute-start.15 = (bf16[2,4,96,768]{3,2,1,0:T(8,128)(2,1)}, bf16[2,4,96,768]{3,2,1,0:T(8,128)(2,1)}, u32[]{:S(2)}, u32[]{:S(2)}) collective-permute-start(bf16[2,4,96,768]{3,2,1,0:T(8,128)(2,1)} %get-tuple-element.102), channel_id=1, source_target_pairs={{0,4},{4,8},{8,12},{12,16},{16,20},{20,24},{24,28},{28,0},{1,5},{5... | collective-permute-start | bytes 3538952 | tf_op jit(solution)/shard_map/ppermute | solution.py:319
  161.0 62.9 %collective-permute-start.16 = (bf16[2,4,96,768]{3,2,1,0:T(8,128)(2,1)}, bf16[2,4,96,768]{3,2,1,0:T(8,128)(2,1)}, u32[]{:S(2)}, u32[]{:S(2)}) collective-permute-start(bf16[2,4,96,768]{3,2,1,0:T(8,128)(2,1)} %get-tuple-element.108), channel_id=1, source_target_pairs={{0,8},{4,12},{8,16},{12,20},{16,24},{20,28},{24,0},{28,4},{1,9},{5... | collective-permute-start | bytes 3538952 | tf_op jit(solution)/shard_map/ppermute | solution.py:319
  162.5 78.4 %collective-permute-start.17 = (bf16[2,4,96,768]{3,2,1,0:T(8,128)(2,1)}, bf16[2,4,96,768]{3,2,1,0:T(8,128)(2,1)}, u32[]{:S(2)}, u32[]{:S(2)}) collective-permute-start(bf16[2,4,96,768]{3,2,1,0:T(8,128)(2,1)} %get-tuple-element.107), channel_id=1, source_target_pairs={{0,12},{4,16},{8,20},{12,24},{16,28},{20,0},{24,4},{28,8},{1,13},{... | collective-permute-start | bytes 3538952 | tf_op jit(solution)/shard_map/ppermute | solution.py:319
  164.0 77.8 %collective-permute-start.18 = (bf16[2,4,96,768]{3,2,1,0:T(8,128)(2,1)}, bf16[2,4,96,768]{3,2,1,0:T(8,128)(2,1)}, u32[]{:S(2)}, u32[]{:S(2)}) collective-permute-start(bf16[2,4,96,768]{3,2,1,0:T(8,128)(2,1)} %get-tuple-element.106), channel_id=1, source_target_pairs={{0,16},{4,20},{8,24},{12,28},{16,0},{20,4},{24,8},{28,12},{1,17},{... | collective-permute-start | bytes 3538952 | tf_op jit(solution)/shard_map/ppermute | solution.py:319
  165.4 103.5 %collective-permute-start.19 = (bf16[2,4,96,768]{3,2,1,0:T(8,128)(2,1)}, bf16[2,4,96,768]{3,2,1,0:T(8,128)(2,1)}, u32[]{:S(2)}, u32[]{:S(2)}) collective-permute-start(bf16[2,4,96,768]{3,2,1,0:T(8,128)(2,1)} %get-tuple-element.105), channel_id=1, source_target_pairs={{0,20},{4,24},{8,28},{12,0},{16,4},{20,8},{24,12},{28,16},{1,21},{... | collective-permute-start | bytes 3538952 | tf_op jit(solution)/shard_map/ppermute | solution.py:319
  221.4 47.4 %collective-permute-start.20 = (bf16[2,4,96,768]{3,2,1,0:T(8,128)(2,1)}, bf16[2,4,96,768]{3,2,1,0:T(8,128)(2,1)}, u32[]{:S(2)}, u32[]{:S(2)}) collective-permute-start(bf16[2,4,96,768]{3,2,1,0:T(8,128)(2,1)} %get-tuple-element.104), channel_id=1, source_target_pairs={{0,24},{4,28},{8,0},{12,4},{16,8},{20,12},{24,16},{28,20},{1,25},{... | collective-permute-start | bytes 3538952 | tf_op jit(solution)/shard_map/ppermute | solution.py:319
  223.9 45.0 %collective-permute-start.21 = (bf16[2,4,96,768]{3,2,1,0:T(8,128)(2,1)}, bf16[2,4,96,768]{3,2,1,0:T(8,128)(2,1)}, u32[]{:S(2)}, u32[]{:S(2)}) collective-permute-start(bf16[2,4,96,768]{3,2,1,0:T(8,128)(2,1)} %get-tuple-element.103), channel_id=1, source_target_pairs={{0,28},{4,0},{8,4},{12,8},{16,12},{20,16},{24,20},{28,24},{1,29},{... | collective-permute-start | bytes 3538952 | tf_op jit(solution)/shard_map/ppermute | solution.py:319
  240.9 34.4 %collective-permute-start.10 = (bf16[128,768]{1,0:T(8,128)(2,1)S(1)}, bf16[128,768]{1,0:T(8,128)(2,1)S(1)}, u32[]{:S(2)}, u32[]{:S(2)}) collective-permute-start(bf16[128,768]{1,0:T(8,128)(2,1)S(1)} %get-tuple-element.114), channel_id=1, source_target_pairs={{0,2},{1,3},{2,0},{3,1},{4,6},{5,7},{6,4},{7,5},{8,10},{9,11},{10,... | collective-permute-start | bytes 589832 | tf_op jit(solution)/shard_map/ppermute | solution.py:132
  241.8 33.6 %collective-permute-start.11 = (bf16[128,768]{1,0:T(8,128)(2,1)S(1)}, bf16[128,768]{1,0:T(8,128)(2,1)S(1)}, u32[]{:S(2)}, u32[]{:S(2)}) collective-permute-start(bf16[128,768]{1,0:T(8,128)(2,1)S(1)} %get-tuple-element.113), channel_id=1, source_target_pairs={{0,3},{1,0},{2,1},{3,2},{4,7},{5,4},{6,5},{7,6},{8,11},{9,8},{10,9... | collective-permute-start | bytes 589832 | tf_op jit(solution)/shard_map/ppermute | solution.py:132
  268.9 9.4 %collective-permute-start.9 = (bf16[128,768]{1,0:T(8,128)(2,1)S(1)}, bf16[128,768]{1,0:T(8,128)(2,1)S(1)}, u32[]{:S(2)}, u32[]{:S(2)}) collective-permute-start(bf16[128,768]{1,0:T(8,128)(2,1)S(1)} %get-tuple-element.112), channel_id=1, source_target_pairs={{0,1},{1,2},{2,3},{3,0},{4,5},{5,6},{6,7},{7,4},{8,9},{9,10},{10,1... | collective-permute-start | bytes 589832 | tf_op jit(solution)/shard_map/ppermute | solution.py:132
  280.8 8.8 %collective-permute-start.12 = (f32[96,6]{1,0:T(8,128)S(1)}, f32[96,6]{1,0:T(8,128)S(1)}, u32[]{:S(2)}, u32[]{:S(2)}) collective-permute-start(f32[96,6]{1,0:T(8,128)S(1)} %slice.168), channel_id=1, source_target_pairs={{0,1},{1,2},{2,3},{3,0},{4,5},{5,6},{6,7},{7,4},{8,9},{9,10},{10,1... | collective-permute-start | bytes 6920 | tf_op jit(solution)/shard_map/ppermute | solution.py:132
  282.3 7.3 %collective-permute-start.13 = (f32[96,6]{1,0:T(8,128)S(1)}, f32[96,6]{1,0:T(8,128)S(1)}, u32[]{:S(2)}, u32[]{:S(2)}) collective-permute-start(f32[96,6]{1,0:T(8,128)S(1)} %slice.168), channel_id=1, source_target_pairs={{0,2},{1,3},{2,0},{3,1},{4,6},{5,7},{6,4},{7,5},{8,10},{9,11},{10,... | collective-permute-start | bytes 6920 | tf_op jit(solution)/shard_map/ppermute | solution.py:132
  284.7 4.9 %collective-permute-start.14 = (f32[96,6]{1,0:T(8,128)S(1)}, f32[96,6]{1,0:T(8,128)S(1)}, u32[]{:S(2)}, u32[]{:S(2)}) collective-permute-start(f32[96,6]{1,0:T(8,128)S(1)} %slice.168), channel_id=1, source_target_pairs={{0,3},{1,0},{2,1},{3,2},{4,7},{5,4},{6,5},{7,6},{8,11},{9,8},{10,9... | collective-permute-start | bytes 6920 | tf_op jit(solution)/shard_map/ppermute | solution.py:132
  (4 other events, 9.4 us)
Sparse Core Ops, SparseCore 0:
  10.5 27.5 all-gather.3
  40.0 38.9 all-gather.5
  80.9 38.9 all-gather.7
  154.3 33.4 reduce-scatter.2
  227.1 52.8 reduce-scatter.4

commit v3 on v2

--- a/solution.py
+++ b/solution.py
@@ -43,7 +43,7 @@
     return ids == buckets
 
 
-def attention_forward(heads, size, tok, gain, wqkv, wout, table, buckets, na, qkv, probs, ctx, part):
+def attention_forward(heads, size, tok, gain, pack, table, buckets, na, qkv, probs, ctx, part):
     length = tok.shape[0]
     wide = 2 * length
     width = heads * size
@@ -51,7 +51,7 @@
     r1 = lax.rsqrt(jnp.mean(x * x, axis=-1, keepdims=True) + EPS)
     rows = (x * r1 * gain[...]).astype(BF)
     na[...] = rows
-    proj = dot(rows, wqkv[...]).astype(BF)
+    proj = dot(rows, pack[:, : 3 * width]).astype(BF)
     qkv[...] = proj
     q, k, v = qkv[:, :width], qkv[:, width : 2 * width], qkv[:, 2 * width :]
     hot = bucket_hot(buckets[...], table.shape[1]).astype(F32).astype(BF)
@@ -76,11 +76,11 @@
         total = total + jnp.where(mask, dot(p.astype(BF), v), 0.0)
     c = total.astype(BF)
     ctx[...] = c
-    part[...] = dot(c, wout[...], 1, 1).astype(BF)
+    part[...] = dot(c, pack[:, 3 * width : 4 * width], 1, 1).astype(BF)
 
 
 def attention_backward(
-    heads, size, tok, na, qkv, probs, ctx, gh, wqkv, wout, gain, buckets, gw, gout, gna, gain_grad, gtable
+    heads, size, tok, na, qkv, probs, ctx, gh, pack, gain, buckets, gw, gout, gna, gain_grad, gtable
 ):
     length = tok.shape[0]
     wide = 2 * length
@@ -88,7 +88,7 @@
     q, k, v = qkv[:, :width], qkv[:, width : 2 * width], qkv[:, 2 * width :]
     g = gh[...]
     gout[...] = dot(g, ctx[...], 0, 0).astype(BF)
-    gctx = dot(g, wout[...]).astype(BF)
+    gctx = dot(g, pack[:, 3 * width : 4 * width]).astype(BF)
     zero = jnp.zeros((length, width), F32)
     gq, gk, gv = zero, zero, zero
     row8 = lax.broadcasted_iota(jnp.int32, (8, wide), 0)
@@ -120,7 +120,7 @@
     grad_na = jnp.zeros((length, tok.shape[1]), F32)
     for i, part in enumerate((gq, gk, gv)):
         gw[i] = dot(rows, part, 0, 0).astype(BF)
-        grad_na = grad_na + dot(part, wqkv[:, i * width : (i + 1) * width], 1, 1)
+        grad_na = grad_na + dot(part, pack[:, i * width : (i + 1) * width], 1, 1)
     gna[...] = grad_na.astype(BF)
     x = tok[...].astype(F32)
     r1 = lax.rsqrt(jnp.mean(x * x, axis=-1, keepdims=True) + EPS)
@@ -228,10 +228,8 @@
     small = jnp.pad(small, ((0, 0), (0, SMALL - small.shape[1])))
     pack = jnp.concatenate([w_query, w_key, w_value, w_output, small], axis=1)
     pack = lax.all_gather(pack, "dp", axis=0, tiled=True)
-    pack, up_full = lax.optimization_barrier((pack, up_full))
     tok_all = gather_rows(tokens)
     cot_all = gather_rows(cotangent)
-    wqkv, wout = pack[:, : 3 * width], pack[:, 3 * width : 4 * width]
     small = pack[:, 4 * width :].astype(F32)
     gain_one = small[:, 0].reshape(1, model)
     gain_two = small[:, 1].reshape(1, model)
@@ -253,8 +251,9 @@
         ),
         3_000_000_000,
         name="attention_forward",
-    )(tok_all, gain_one, wqkv, wout, table8, bucket_row)
+    )(tok_all, gain_one, pack, table8, bucket_row)
     attended = scatter_rows(part)
+    attended, up_full = lax.optimization_barrier((attended, up_full))
 
     token_rows = tokens.astype(F32)
     hidden = token_rows + attended
@@ -351,7 +350,7 @@
         ),
         4_000_000_000,
         name="attention_backward",
-    )(tok_all, na, qkv, probs, ctx, gh_all, wqkv, wout, gain_one, bucket_row)
+    )(tok_all, na, qkv, probs, ctx, gh_all, pack, gain_one, bucket_row)
     grad_na = scatter_rows(gna)
     r1 = lax.rsqrt(jnp.mean(token_rows * token_rows, axis=-1, keepdims=True) + EPS)
     u1 = token_rows * r1

time: 298 us -> 282 us (0.946)
  waiting for transfers between devices: 129 us -> 100 us
  starting transfers between devices: 30.3 us -> 40.7 us
  matrix products: 1.58 us -> 4.67 us
    all_gather x1, waiting for transfers between devices: 40.9 us -> 9.17 us  [per_device(): up_full = lax.all_gather(expert_up, 'dp', axis=1, tiled=True)]
    all_gather x1, waiting for transfers between devices: 0.01 us -> 15.4 us  [per_device(): down_full = lax.all_gather(expert_down, 'dp', axis=1, tiled=True)]
    ppermute x15, starting transfers between devices: 23.3 us -> 33.8 us  [turn(): return lax.ppermute(x, 'tensor', [(i, (i + k) % n) for i in range(n)])]
    ppermute x7, waiting for transfers between devices: 39 us -> 29.9 us  [per_device(): traded.append(lax.ppermute(piece, 'dp', pairs))]
    ppermute x15, waiting for transfers between devices: 23.5 us -> 17.3 us  [turn(): return lax.ppermute(x, 'tensor', [(i, (i + k) % n) for i in range(n)])]
    slice x2 -> x0, local copies, waits for them, and re-layouts: 3.15 us -> none  [per_device(): wqkv, wout = (pack[:, :3 * width], pack[:, 3 * width:4 * width])]
  transfers between devices with their start and end apart: 27 -> 27, of which waited for: 10 -> 11; matrix products, arithmetic and copies ran while one was open for 14% -> 16% of each run, Pallas kernels for 5% -> 6%
where the time goes in v3:
time: 282 us; the launch traced here: 281 us
  waiting for transfers between devices  100 us (35%)
  starting transfers between devices  40.7 us (14%)
  blocking collectives  39.7 us (14%)
  Pallas kernels  32.3 us (11%)
  local copies, waits for them, and re-layouts  30.2 us (11%)
  other arithmetic  19.2 us (7%)
  between operations  14.2 us (5%)
  matrix products  4.67 us (2%)
    ppermute x15, starting transfers between devices, turn(): return lax.ppermute(x, 'tensor', [(i, (i + k) % n) for i in range(n)])  33.8 us
    ppermute x7, waiting for transfers between devices, per_device(): traded.append(lax.ppermute(piece, 'dp', pairs))  29.9 us
    reduce_scatter x1, waiting for transfers between devices, per_device(): lax.psum_scatter(jnp.concatenate([ret, gnf], axis=1), 'tensor', scatter_d...  24.3 us
    all_gather x1, blocking collectives, per_device(): lax.all_gather(jnp.concatenate([nf.astype(BF), gate_cols], axis=1), 'tens...  21 us
    all_gather x1, blocking collectives, per_device(): lax.all_gather(grad_hidden.astype(BF), 'tensor', axis=0, tiled=True)  18.7 us
    ppermute x15, waiting for transfers between devices, turn(): return lax.ppermute(x, 'tensor', [(i, (i + k) % n) for i in range(n)])  17.3 us
    pallas_call x1, Pallas kernels, per_device(): call(lambda *refs: ffn_kernel(CAP, cut, *refs), (sds((length, model)), sd...  15.7 us
    all_gather x1, waiting for transfers between devices, per_device(): down_full = lax.all_gather(expert_down, 'dp', axis=1, tiled=True)  15.4 us
  transfers between devices with their start and end apart: 27, of which 11 were waited for; matrix products, arithmetic and copies ran while one was open for 16% of the time, Pallas kernels for 6%

profile of v3, /device:TPU:0, one launch (start us, length us, event | category | flops | bytes accessed | tf_op | source)
XLA Modules:
  0.0 281.3 jit_solution(4323280218068225292)
XLA Ops:
  8.2 1.7 concatenate.23
  11.5 3.1 %collective-permute-start = (bf16[128,768]{1,0:T(8,128)(2,1)S(1)}, bf16[128,768]{1,0:T(8,128)(2,1)S(1)}, u32[]{:S(2)}, u32[]{:S(2)}) collective-permute-start(bf16[128,768]{1,0:T(8,128)(2,1)S(1)} %copy-done), channel_id=1, source_target_pairs={{0,1},{1,2},{2,3},{3,0},{4,5},{5,6},{6,7},{7,4},{8,9},{9,10},{10,1... | collective-permute-start | bytes 589832 | tf_op jit(solution)/shard_map/ppermute | solution.py:132
  14.6 2.6 collective-permute-start.1
  22.4 2.5 collective-permute-start.8
  25.0 10.2 %collective-permute-done.6 = bf16[128,768]{1,0:T(8,128)(2,1)S(1)} collective-permute-done((bf16[128,768]{1,0:T(8,128)(2,1)S(1)}, bf16[128,768]{1,0:T(8,128)(2,1)S(1)}, u32[]{:S(2)}, u32[]{:S(2)}) %collective-permute-start.6) | collective-permute-done | bytes 196640 | tf_op jit(solution)/shard_map/ppermute | solution.py:132
  35.2 2.9 %all-gather.4.cloned.1.call-done.refs_2_.refs_6_ = bf16[768,896]{1,0:T(8,128)(2,1)} async-done(((bf16[96,896]{1,0:T(8,128)(2,1)}), bf16[768,896]{1,0:T(8,128)(2,1)}) %all-gather.4.cloned.1.call-update) | async-done | bytes 1376272 | tf_op jit(solution)/shard_map/all_gather | solution.py:230
  40.1 6.8 %attention_forward.1 = (bf16[512,768]{1,0:T(8,128)(2,1)}, bf16[512,576]{1,0:T(8,128)(2,1)}, f32[3,512,512]{2,1,0:T(8,128)}, bf16[512,192]{1,0:T(8,128)(2,1)}, bf16[512,768]{1,0:T(8,128)(2,1)}) custom-call(bf16[512,768]{1,0:T(8,128)(2,1)} %copy-done.7, f32[1,768]{1,0:T(1,128)} %reshape_squeeze.7.refs_1_.refs_7_, ...), custom_call_target="tpu_custom_call" | custom-call | flops 3000000000 | bytes 12000000 | tf_op jit(solution)/shard_map/attention_forward/pallas_call | solution.py:243
  48.1 9.1 %collective-permute-start.3 = (bf16[128,768]{1,0:T(8,128)(2,1)S(1)}, bf16[128,768]{1,0:T(8,128)(2,1)S(1)}, u32[]{:S(2)}, u32[]{:S(2)}) collective-permute-start(bf16[128,768]{1,0:T(8,128)(2,1)S(1)} %get-tuple-element.117), channel_id=1, source_target_pairs={{0,1},{1,2},{2,3},{3,0},{4,5},{5,6},{6,7},{7,4},{8,9},{9,10},{10,1... | collective-permute-start | bytes 589832 | tf_op jit(solution)/shard_map/ppermute | solution.py:132
  57.2 2.0 collective-permute-start.4
  59.1 2.8 %collective-permute-start.5 = (bf16[128,768]{1,0:T(8,128)(2,1)S(1)}, bf16[128,768]{1,0:T(8,128)(2,1)S(1)}, u32[]{:S(2)}, u32[]{:S(2)}) collective-permute-start(bf16[128,768]{1,0:T(8,128)(2,1)S(1)} %get-tuple-element.118), channel_id=1, source_target_pairs={{0,3},{1,0},{2,1},{3,2},{4,7},{5,4},{6,5},{7,6},{8,11},{9,8},{10,9... | collective-permute-start | bytes 589832 | tf_op jit(solution)/shard_map/ppermute | solution.py:132
  62.5 6.3 %collective-permute-done.4 = bf16[128,768]{1,0:T(8,128)(2,1)S(1)} collective-permute-done((bf16[128,768]{1,0:T(8,128)(2,1)S(1)}, bf16[128,768]{1,0:T(8,128)(2,1)S(1)}, u32[]{:S(2)}, u32[]{:S(2)}) %collective-permute-start.4) | collective-permute-done | bytes 196640 | tf_op jit(solution)/shard_map/ppermute | solution.py:132
  69.8 9.2 %all-gather.6.cloned.1.call-done.refs_4_ = bf16[4,768,768]{2,1,0:T(8,128)(2,1)} async-done(((bf16[4,96,768]{2,1,0:T(8,128)(2,1)}), bf16[4,768,768]{2,1,0:T(8,128)(2,1)}) %all-gather.6.cloned.1.call-update) | async-done | bytes 4718608 | tf_op jit(solution)/shard_map/all_gather | solution.py:225
  81.5 21.0 %all_gather.17 = bf16[512,896]{1,0:T(8,128)(2,1)S(1)} all-gather(bf16[128,896]{1,0:T(8,128)(2,1)S(1)} %fusion.14), channel_id=1, replica_groups=mesh['dp'=8,'tensor'=4] {'tensor'}, dimensions={0}, use_global_device_ids=true | all-gather | bytes 1146880 | tf_op jit(solution)/shard_map/all_gather | solution.py:273
  104.4 15.4 %all-gather.8.cloned.1.call-done.refs_5_ = bf16[4,768,768]{2,1,0:T(8,128)(2,1)} async-done(((bf16[4,96,768]{2,1,0:T(8,128)(2,1)}), bf16[4,768,768]{2,1,0:T(8,128)(2,1)}) %all-gather.8.cloned.1.call-update) | async-done | bytes 4718608 | tf_op jit(solution)/shard_map/all_gather | solution.py:226
  119.8 15.7 %experts.1 = (bf16[512,768]{1,0:T(8,128)(2,1)}, bf16[512,768]{1,0:T(8,128)(2,1)}, bf16[8,2,4,96,768]{4,3,2,1,0:T(8,128)(2,1)}) custom-call(s32[1,512]{1,0:T(1,128)} %bitcast.121, bf16[512,768]{1,0:T(8,128)(2,1)} %slice.158.refs_1_, f32[512,1]{1,0:T(8,128)} %copy.52.refs_2_, bf16[512,768]{1,0:T(8,128)(2,1)} %copy-done.6, ...), custom_call_target="tpu_custom_call" | custom-call | flops 6000000000 | bytes 12000000 | tf_op jit(solution)/shard_map/experts/pallas_call | solution.py:288
  135.5 2.6 pad_maximum_fusion
  138.3 6.7 %dynamic-slice_bitcast_fusion.6 = (bf16[2,4,96,768]{3,2,1,0:T(8,128)(2,1)}, bf16[2,4,96,768]{3,2,1,0:T(8,128)(2,1)}, bf16[2,4,96,768]{3,2,1,0:T(8,128)(2,1)}, bf...) fusion(bf16[8,2,4,96,768]{4,3,2,1,0:T(8,128)(2,1)} %get-tuple-e, ...), kind=kLoop, calls=%fused_computation.22 | loop fusion | bytes 16515100 | tf_op jit(solution)/shard_map/jit(dynamic_index_in_dim)/squeeze | solution.py:316
  147.9 1.5 collective-permute-start.18
  149.4 24.3 %reduce-scatter.3.cloned.1.call-done = bf16[128,1536]{1,0:T(8,128)(2,1)} async-done(((bf16[512,1536]{1,0:T(8,128)(2,1)}), bf16[128,1536]{1,0:T(8,128)(2,1)}) %reduce-scatter.3.cloned.1.call-update) | async-done | bytes 393232 | tf_op jit(solution)/shard_map/reduce_scatter | solution.py:323
  175.5 2.2 multiply_reduce_fusion
  180.4 18.7 %all_gather.19.refs_5_ = bf16[512,768]{1,0:T(8,128)(2,1)} all-gather(bf16[128,768]{1,0:T(8,128)(2,1)} %fusion.31), channel_id=1, replica_groups=mesh['dp'=8,'tensor'=4] {'tensor'}, dimensions={0}, use_global_device_ids=true | all-gather | bytes 983040 | tf_op jit(solution)/shard_map/all_gather | solution.py:340
  199.1 9.8 %attention_backward.1 = (bf16[3,768,192]{2,1,0:T(8,128)(2,1)}, bf16[768,192]{1,0:T(8,128)(2,1)}, bf16[512,768]{1,0:T(8,128)(2,1)}, f32[1,768]{1,0:T(1,128)}, f32[8,32]{1,0:T(8,128)}) custom-call(bf16[512,768]{1,0:T(8,128)(2,1)} %copy-done.7, bf16[512,768]{1,0:T(8,128)(2,1)} %get-tuple-element.32.refs_1_, bf16[512,576]{1,0:T(8,128)(2,1)} %get-tuple-element.33.refs_2_, ...), custom_call_target="tpu_custom_call" | custom-call | flops 4000000000 | bytes 12000000 | tf_op jit(solution)/shard_map/attention_backward/pallas_call | solution.py:342
  214.7 2.4 collective-permute-start.20
  218.2 3.3 %concatenate.28 = bf16[768,896]{1,0:T(8,128)(2,1)} concatenate(bf16[768,192]{1,0:T(8,128)(2,1)S(1)} %get-tuple-element.111, bf16[768,192]{1,0:T(8,128)(2,1)S(1)} %get-tuple-element.110, bf16[768,192]{1,0:T(8,128)(2,1)S(1)} %get-tuple-element.109, bf16[768,192]{1,0:T(8,128)(2,1)} %get-tuple-element.38, bf16[768,128]{1,0:T(8,128)(2,1)} %pad.25), dimensions={1} | concatenate | bytes 2752512 | tf_op jit(solution)/shard_map/concatenate | solution.py:366
  222.6 2.3 collective-permute-done.17
  224.9 2.4 collective-permute-start.10
  228.7 24.0 %collective-permute-done.19 = bf16[2,4,96,768]{3,2,1,0:T(8,128)(2,1)} collective-permute-done((bf16[2,4,96,768]{3,2,1,0:T(8,128)(2,1)}, bf16[2,4,96,768]{3,2,1,0:T(8,128)(2,1)}, u32[]{:S(2)}, u32[]{:S(2)}) %collective-permute-start.19) | collective-permute-done | bytes 1179680 | tf_op jit(solution)/shard_map/ppermute | solution.py:318
  252.8 1.5 collective-permute-start.9
  254.3 3.5 %collective-permute-done.21 = bf16[2,4,96,768]{3,2,1,0:T(8,128)(2,1)} collective-permute-done((bf16[2,4,96,768]{3,2,1,0:T(8,128)(2,1)}, bf16[2,4,96,768]{3,2,1,0:T(8,128)(2,1)}, u32[]{:S(2)}, u32[]{:S(2)}) %collective-permute-start.21) | collective-permute-done | bytes 1179680 | tf_op jit(solution)/shard_map/ppermute | solution.py:318
  257.8 5.9 %convert_add_fusion = (f32[4,96,768]{2,1,0:T(8,128)}, f32[4,96,768]{2,1,0:T(8,128)}) fusion(bf16[2,4,96,768]{3,2,1,0:T(8,128)(2,1)} %collective-permute-done.21, bf16[2,4,96,768]{3,2,1,0:T(8,128)(2,1)} %collective-permute-done.20, bf16[2,4,96,768]{3,2,1,0:T(8,128)(2,1)} %collective-permute-done.19, bf16[2,4,96,768]{3,2,1,0:T(8,128)(2,1)} %collective-permute-done.18, ...), kind=kLoop, calls=%fused_computation.2 | loop fusion | flops 8847360 | bytes 11796488 | tf_op jit(solution)/shard_map/add | solution.py:381
  265.8 2.7 collective-permute-start.13
  270.8 1.7 fusion.33
  (146 shorter events, 40.4 us)
Async XLA Ops:
  7.2 30.9 %all-gather.4.cloned.1.call-start = ((), (), s32[]{:S(2)}) async-start(), calls=%async_computation.2 | async-start | bytes 1548288 | tf_op jit(solution)/shard_map/all_gather | solution.py:230
  9.9 69.0 %all-gather.6.cloned.1.call-start = ((), (), s32[]{:S(2)}) async-start(), calls=%async_computation.3 | async-start | bytes 5308416 | tf_op jit(solution)/shard_map/all_gather | solution.py:225
  10.7 109.1 %all-gather.8.cloned.1.call-start = ((), (), s32[]{:S(2)}) async-start(), calls=%async_computation.4 | async-start | bytes 5308416 | tf_op jit(solution)/shard_map/all_gather | solution.py:226
  11.4 162.2 %reduce-scatter.3.cloned.1.call-start = ((), (), s32[]{:S(2)}) async-start(), calls=%async_computation.5 | async-start | bytes 1966080 | tf_op jit(solution)/shard_map/reduce_scatter | solution.py:323
  11.5 11.0 %collective-permute-start = (bf16[128,768]{1,0:T(8,128)(2,1)S(1)}, bf16[128,768]{1,0:T(8,128)(2,1)S(1)}, u32[]{:S(2)}, u32[]{:S(2)}) collective-permute-start(bf16[128,768]{1,0:T(8,128)(2,1)S(1)} %copy-done), channel_id=1, source_target_pairs={{0,1},{1,2},{2,3},{3,0},{4,5},{5,6},{6,7},{7,4},{8,9},{9,10},{10,1... | collective-permute-start | bytes 589832 | tf_op jit(solution)/shard_map/ppermute | solution.py:132
  14.6 20.6 %collective-permute-start.1 = (bf16[128,768]{1,0:T(8,128)(2,1)S(1)}, bf16[128,768]{1,0:T(8,128)(2,1)S(1)}, u32[]{:S(2)}, u32[]{:S(2)}) collective-permute-start(bf16[128,768]{1,0:T(8,128)(2,1)S(1)} %copy-done), channel_id=1, source_target_pairs={{0,2},{1,3},{2,0},{3,1},{4,6},{5,7},{6,4},{7,5},{8,10},{9,11},{10,... | collective-permute-start | bytes 589832 | tf_op jit(solution)/shard_map/ppermute | solution.py:132
  17.1 18.0 %collective-permute-start.2 = (bf16[128,768]{1,0:T(8,128)(2,1)S(1)}, bf16[128,768]{1,0:T(8,128)(2,1)S(1)}, u32[]{:S(2)}, u32[]{:S(2)}) collective-permute-start(bf16[128,768]{1,0:T(8,128)(2,1)S(1)} %copy-done), channel_id=1, source_target_pairs={{0,3},{1,0},{2,1},{3,2},{4,7},{5,4},{6,5},{7,6},{8,11},{9,8},{10,9... | collective-permute-start | bytes 589832 | tf_op jit(solution)/shard_map/ppermute | solution.py:132
  18.5 16.6 %collective-permute-start.6 = (bf16[128,768]{1,0:T(8,128)(2,1)S(1)}, bf16[128,768]{1,0:T(8,128)(2,1)S(1)}, u32[]{:S(2)}, u32[]{:S(2)}) collective-permute-start(bf16[128,768]{1,0:T(8,128)(2,1)S(1)} %copy-done.1), channel_id=1, source_target_pairs={{0,1},{1,2},{2,3},{3,0},{4,5},{5,6},{6,7},{7,4},{8,9},{9,10},{10,1... | collective-permute-start | bytes 589832 | tf_op jit(solution)/shard_map/ppermute | solution.py:132
  19.2 42.8 %collective-permute-start.7 = (bf16[128,768]{1,0:T(8,128)(2,1)S(1)}, bf16[128,768]{1,0:T(8,128)(2,1)S(1)}, u32[]{:S(2)}, u32[]{:S(2)}) collective-permute-start(bf16[128,768]{1,0:T(8,128)(2,1)S(1)} %copy-done.1), channel_id=1, source_target_pairs={{0,2},{1,3},{2,0},{3,1},{4,6},{5,7},{6,4},{7,5},{8,10},{9,11},{10,... | collective-permute-start | bytes 589832 | tf_op jit(solution)/shard_map/ppermute | solution.py:132
  22.4 39.6 %collective-permute-start.8 = (bf16[128,768]{1,0:T(8,128)(2,1)S(1)}, bf16[128,768]{1,0:T(8,128)(2,1)S(1)}, u32[]{:S(2)}, u32[]{:S(2)}) collective-permute-start(bf16[128,768]{1,0:T(8,128)(2,1)S(1)} %copy-done.1), channel_id=1, source_target_pairs={{0,3},{1,0},{2,1},{3,2},{4,7},{5,4},{6,5},{7,6},{8,11},{9,8},{10,9... | collective-permute-start | bytes 589832 | tf_op jit(solution)/shard_map/ppermute | solution.py:132
  48.1 14.4 %collective-permute-start.3 = (bf16[128,768]{1,0:T(8,128)(2,1)S(1)}, bf16[128,768]{1,0:T(8,128)(2,1)S(1)}, u32[]{:S(2)}, u32[]{:S(2)}) collective-permute-start(bf16[128,768]{1,0:T(8,128)(2,1)S(1)} %get-tuple-element.117), channel_id=1, source_target_pairs={{0,1},{1,2},{2,3},{3,0},{4,5},{5,6},{6,7},{7,4},{8,9},{9,10},{10,1... | collective-permute-start | bytes 589832 | tf_op jit(solution)/shard_map/ppermute | solution.py:132
  57.2 11.6 %collective-permute-start.4 = (bf16[128,768]{1,0:T(8,128)(2,1)S(1)}, bf16[128,768]{1,0:T(8,128)(2,1)S(1)}, u32[]{:S(2)}, u32[]{:S(2)}) collective-permute-start(bf16[128,768]{1,0:T(8,128)(2,1)S(1)} %get-tuple-element.119), channel_id=1, source_target_pairs={{0,2},{1,3},{2,0},{3,1},{4,6},{5,7},{6,4},{7,5},{8,10},{9,11},{10,... | collective-permute-start | bytes 589832 | tf_op jit(solution)/shard_map/ppermute | solution.py:132
  59.1 9.6 %collective-permute-start.5 = (bf16[128,768]{1,0:T(8,128)(2,1)S(1)}, bf16[128,768]{1,0:T(8,128)(2,1)S(1)}, u32[]{:S(2)}, u32[]{:S(2)}) collective-permute-start(bf16[128,768]{1,0:T(8,128)(2,1)S(1)} %get-tuple-element.118), channel_id=1, source_target_pairs={{0,3},{1,0},{2,1},{3,2},{4,7},{5,4},{6,5},{7,6},{8,11},{9,8},{10,9... | collective-permute-start | bytes 589832 | tf_op jit(solution)/shard_map/ppermute | solution.py:132
  62.1 19.1 %copy-start.15 = (s32[128]{0:T(128)S(1)}, s32[128]{0:T(128)}, u32[]{:S(2)}) copy-start(s32[128]{0:T(128)} %fusion.29) | copy-start | bytes 1540
  79.6 98.1 %copy-start.8 = (f32[128]{0:T(128)}, f32[128]{0:T(128)S(1)}, u32[]{:S(2)}) copy-start(f32[128]{0:T(128)S(1)} %add_rsqrt_fusion.1) | copy-start | bytes 1540
  81.2 93.5 %copy-start.12 = (f32[128]{0:T(128)}, f32[128]{0:T(128)S(1)}, u32[]{:S(2)}) copy-start(f32[128]{0:T(128)S(1)} %get-tuple-element.96) | copy-start | bytes 1540
  81.2 94.3 %copy-start.10 = (f32[128,4]{0,1:T(4,128)}, f32[128,4]{0,1:T(4,128)S(1)}, u32[]{:S(2)}) copy-start(f32[128,4]{0,1:T(4,128)S(1)} %get-tuple-element.97) | copy-start | bytes 6148
  138.2 126.9 %reduce-scatter.5.cloned.1.call-start = ((), (), s32[]{:S(2)}) async-start(), calls=%async_computation.6 | async-start | bytes 1548288 | tf_op jit(solution)/shard_map/reduce_scatter | solution.py:365
  145.0 69.7 %collective-permute-start.15 = (bf16[2,4,96,768]{3,2,1,0:T(8,128)(2,1)}, bf16[2,4,96,768]{3,2,1,0:T(8,128)(2,1)S(1)}, u32[]{:S(2)}, u32[]{:S(2)}) collective-permute-start(bf16[2,4,96,768]{3,2,1,0:T(8,128)(2,1)} %get-tuple-element.102), channel_id=1, source_target_pairs={{0,4},{4,8},{8,12},{12,16},{16,20},{20,24},{24,28},{28,0},{1,5},{5... | collective-permute-start | bytes 3538952 | tf_op jit(solution)/shard_map/ppermute | solution.py:318
  145.3 71.8 %collective-permute-start.16 = (bf16[2,4,96,768]{3,2,1,0:T(8,128)(2,1)}, bf16[2,4,96,768]{3,2,1,0:T(8,128)(2,1)S(1)}, u32[]{:S(2)}, u32[]{:S(2)}) collective-permute-start(bf16[2,4,96,768]{3,2,1,0:T(8,128)(2,1)} %get-tuple-element.108), channel_id=1, source_target_pairs={{0,8},{4,12},{8,16},{12,20},{16,24},{20,28},{24,0},{28,4},{1,9},{5... | collective-permute-start | bytes 3538952 | tf_op jit(solution)/shard_map/ppermute | solution.py:318
  146.7 78.3 %collective-permute-start.17 = (bf16[2,4,96,768]{3,2,1,0:T(8,128)(2,1)}, bf16[2,4,96,768]{3,2,1,0:T(8,128)(2,1)}, u32[]{:S(2)}, u32[]{:S(2)}) collective-permute-start(bf16[2,4,96,768]{3,2,1,0:T(8,128)(2,1)} %get-tuple-element.107), channel_id=1, source_target_pairs={{0,12},{4,16},{8,20},{12,24},{16,28},{20,0},{24,4},{28,8},{1,13},{... | collective-permute-start | bytes 3538952 | tf_op jit(solution)/shard_map/ppermute | solution.py:318
  147.9 79.5 %collective-permute-start.18 = (bf16[2,4,96,768]{3,2,1,0:T(8,128)(2,1)}, bf16[2,4,96,768]{3,2,1,0:T(8,128)(2,1)}, u32[]{:S(2)}, u32[]{:S(2)}) collective-permute-start(bf16[2,4,96,768]{3,2,1,0:T(8,128)(2,1)} %get-tuple-element.106), channel_id=1, source_target_pairs={{0,16},{4,20},{8,24},{12,28},{16,0},{20,4},{24,8},{28,12},{1,17},{... | collective-permute-start | bytes 3538952 | tf_op jit(solution)/shard_map/ppermute | solution.py:318
  149.3 103.4 %collective-permute-start.19 = (bf16[2,4,96,768]{3,2,1,0:T(8,128)(2,1)}, bf16[2,4,96,768]{3,2,1,0:T(8,128)(2,1)}, u32[]{:S(2)}, u32[]{:S(2)}) collective-permute-start(bf16[2,4,96,768]{3,2,1,0:T(8,128)(2,1)} %get-tuple-element.105), channel_id=1, source_target_pairs={{0,20},{4,24},{8,28},{12,0},{16,4},{20,8},{24,12},{28,16},{1,21},{... | collective-permute-start | bytes 3538952 | tf_op jit(solution)/shard_map/ppermute | solution.py:318
  214.7 39.6 %collective-permute-start.20 = (bf16[2,4,96,768]{3,2,1,0:T(8,128)(2,1)}, bf16[2,4,96,768]{3,2,1,0:T(8,128)(2,1)}, u32[]{:S(2)}, u32[]{:S(2)}) collective-permute-start(bf16[2,4,96,768]{3,2,1,0:T(8,128)(2,1)} %get-tuple-element.104), channel_id=1, source_target_pairs={{0,24},{4,28},{8,0},{12,4},{16,8},{20,12},{24,16},{28,20},{1,25},{... | collective-permute-start | bytes 3538952 | tf_op jit(solution)/shard_map/ppermute | solution.py:318
  217.1 40.7 %collective-permute-start.21 = (bf16[2,4,96,768]{3,2,1,0:T(8,128)(2,1)}, bf16[2,4,96,768]{3,2,1,0:T(8,128)(2,1)}, u32[]{:S(2)}, u32[]{:S(2)}) collective-permute-start(bf16[2,4,96,768]{3,2,1,0:T(8,128)(2,1)} %get-tuple-element.103), channel_id=1, source_target_pairs={{0,28},{4,0},{8,4},{12,8},{16,12},{20,16},{24,20},{28,24},{1,29},{... | collective-permute-start | bytes 3538952 | tf_op jit(solution)/shard_map/ppermute | solution.py:318
  221.5 36.3 %copy-start.4 = (bf16[2,4,96,768]{3,2,1,0:T(8,128)(2,1)S(1)}, bf16[2,4,96,768]{3,2,1,0:T(8,128)(2,1)}, u32[]{:S(2)}) copy-start(bf16[2,4,96,768]{3,2,1,0:T(8,128)(2,1)} %copy-done.3) | copy-start | bytes 3538948
  224.9 38.7 %collective-permute-start.10 = (bf16[128,768]{1,0:T(8,128)(2,1)S(1)}, bf16[128,768]{1,0:T(8,128)(2,1)S(1)}, u32[]{:S(2)}, u32[]{:S(2)}) collective-permute-start(bf16[128,768]{1,0:T(8,128)(2,1)S(1)} %get-tuple-element.114), channel_id=1, source_target_pairs={{0,2},{1,3},{2,0},{3,1},{4,6},{5,7},{6,4},{7,5},{8,10},{9,11},{10,... | collective-permute-start | bytes 589832 | tf_op jit(solution)/shard_map/ppermute | solution.py:132
  227.3 36.3 %collective-permute-start.11 = (bf16[128,768]{1,0:T(8,128)(2,1)S(1)}, bf16[128,768]{1,0:T(8,128)(2,1)S(1)}, u32[]{:S(2)}, u32[]{:S(2)}) collective-permute-start(bf16[128,768]{1,0:T(8,128)(2,1)S(1)} %get-tuple-element.113), channel_id=1, source_target_pairs={{0,3},{1,0},{2,1},{3,2},{4,7},{5,4},{6,5},{7,6},{8,11},{9,8},{10,9... | collective-permute-start | bytes 589832 | tf_op jit(solution)/shard_map/ppermute | solution.py:132
  252.8 10.9 %collective-permute-start.9 = (bf16[128,768]{1,0:T(8,128)(2,1)S(1)}, bf16[128,768]{1,0:T(8,128)(2,1)S(1)}, u32[]{:S(2)}, u32[]{:S(2)}) collective-permute-start(bf16[128,768]{1,0:T(8,128)(2,1)S(1)} %get-tuple-element.112), channel_id=1, source_target_pairs={{0,1},{1,2},{2,3},{3,0},{4,5},{5,6},{6,7},{7,4},{8,9},{9,10},{10,1... | collective-permute-start | bytes 589832 | tf_op jit(solution)/shard_map/ppermute | solution.py:132
  265.8 7.5 %collective-permute-start.12 = (f32[96,6]{1,0:T(8,128)S(1)}, f32[96,6]{1,0:T(8,128)S(1)}, u32[]{:S(2)}, u32[]{:S(2)}) collective-permute-start(f32[96,6]{1,0:T(8,128)S(1)} %slice.162), channel_id=1, source_target_pairs={{0,1},{1,2},{2,3},{3,0},{4,5},{5,6},{6,7},{7,4},{8,9},{9,10},{10,1... | collective-permute-start | bytes 6920 | tf_op jit(solution)/shard_map/ppermute | solution.py:132
  265.8 7.5 %collective-permute-start.13 = (f32[96,6]{1,0:T(8,128)S(1)}, f32[96,6]{1,0:T(8,128)S(1)}, u32[]{:S(2)}, u32[]{:S(2)}) collective-permute-start(f32[96,6]{1,0:T(8,128)S(1)} %slice.162), channel_id=1, source_target_pairs={{0,2},{1,3},{2,0},{3,1},{4,6},{5,7},{6,4},{7,5},{8,10},{9,11},{10,... | collective-permute-start | bytes 6920 | tf_op jit(solution)/shard_map/ppermute | solution.py:132
  268.5 4.8 %collective-permute-start.14 = (f32[96,6]{1,0:T(8,128)S(1)}, f32[96,6]{1,0:T(8,128)S(1)}, u32[]{:S(2)}, u32[]{:S(2)}) collective-permute-start(f32[96,6]{1,0:T(8,128)S(1)} %slice.162), channel_id=1, source_target_pairs={{0,3},{1,0},{2,1},{3,2},{4,7},{5,4},{6,5},{7,6},{8,11},{9,8},{10,9... | collective-permute-start | bytes 6920 | tf_op jit(solution)/shard_map/ppermute | solution.py:132
  (17 other events, 116.7 us)
Sparse Core Ops, SparseCore 0:
  10.5 27.5 all-gather.3
  40.0 38.9 all-gather.5
  80.9 38.9 all-gather.7
  138.3 35.2 reduce-scatter.2
  221.6 38.3 reduce-scatter.4
